TPU v7x, 512 devices: a whole 4x4x16 slice. The times are simulated.
512 devices in a mesh: row: 32 (over x_lo, z), col: 16 (over x_hi, y, core).
Axes of the slice: x: 4 (x_hi: 2, x_lo: 2; x = x_hi * 2 + x_lo), y: 4, z: 16, core: 2. Of those that a mesh axis runs over, the one named last changes fastest.
Arguments:
- train_codes: bfloat16 [16384, 32768], P('row', 'col'), may hold values from -6 to 6
- train_exps: int32 [16384, 256], P('row', 'col'), may hold values from -3 to 3
- train_ids: int32 [16384], P('row'), may hold values from 0 to 63
- query_codes: bfloat16 [2048, 32768], P('row', 'col'), may hold values from -6 to 6
- query_exps: int32 [2048, 256], P('row', 'col'), may hold values from -3 to 3
- query_ids: int32 [2048], P('row'), may hold values from 0 to 63
- precond: float32 [32768], P('col'), may hold values from 0.1 to 10
Outputs:
- cosines: float32 [16384, 2048], P('row', 'col')
- peak: float32 [16384], P('row')
All inputs are finite; a program needn't handle non-finite values.
Results may differ from a plain program's by a relative error of at most 0.0045.
Values may be sent and summed in bfloat16 or wider, within the bound.
A program may use at most 64 MiB of HBM per device.

v0:
```python
import math

import jax
import jax.numpy as jnp
from jax import lax
from jax.sharding import PartitionSpec as P

P_SIZE = 32768


epsilon = 1e-06


def dequantize(codes, exps):
    count = codes.shape[0]
    blocks = exps.shape[1]
    factor = jnp.exp2(exps.astype(jnp.float32)).astype(jnp.bfloat16)
    shaped = codes.reshape(count, blocks, codes.shape[1] // blocks) * factor[:, :, None]
    return shaped.reshape(count, codes.shape[1])


def precondition(codes, exps, precond):
    count = codes.shape[0]
    blocks = exps.shape[1]
    factor = jnp.exp2(exps.astype(jnp.float32))
    shaped = (
        codes.astype(jnp.float32).reshape(count, blocks, codes.shape[1] // blocks)
        * factor[:, :, None]
    )
    return (shaped.reshape(count, codes.shape[1]) * precond[None, :]).astype(jnp.bfloat16)


def squares(values):
    return jnp.sum(jnp.square(values.astype(jnp.float32)), axis=1)


def similarity(raw, train_sq, query_sq, train_ids, query_ids):
    denom = jnp.sqrt((train_sq[:, None] + epsilon) * (query_sq[None, :] + epsilon))
    value = math.sqrt(P_SIZE) * raw / denom
    return jnp.where(train_ids[:, None] == query_ids[None, :], jnp.float32(0.0), value)


def shards(train_codes, train_exps, train_ids, query_codes, query_exps, query_ids, precond):
    train_grad = dequantize(train_codes, train_exps)
    query_pre = precondition(query_codes, query_exps, precond)
    train_part = squares(train_grad)
    gathered, every_id = (
        lax.all_gather(query_pre, "row", axis=0, tiled=True),
        lax.all_gather(query_ids, "row", axis=0, tiled=True),
    )
    train_sq, query_sq = lax.psum((train_part, squares(gathered)), "col")
    raw_part = jnp.einsum("tf,qf->tq", train_grad, gathered, preferred_element_type=jnp.float32)
    share = raw_part.shape[1] // lax.axis_size("col")
    start = lax.axis_index("col") * share
    raw = lax.psum(raw_part, "col")
    whole = similarity(raw, train_sq, query_sq, train_ids, every_id)
    peak = jnp.max(whole, axis=1)
    block_out = lax.dynamic_slice_in_dim(whole, start, share, 1)
    return (block_out, peak)


def solution(mesh):
    in_specs = (
        P("row", "col"),
        P("row", "col"),
        P("row"),
        P("row", "col"),
        P("row", "col"),
        P("row"),
        P("col"),
    )
    out_specs = (P("row", "col"), P("row"))
    return jax.shard_map(shards, mesh=mesh, in_specs=in_specs, out_specs=out_specs, check_vma=False)
```

profile of v0, /device:TPU:1, one launch (start us, length us, event | category | flops | bytes accessed | tf_op | source)
XLA Modules:
  0.0 348.3 jit_solution(3827443655980024571)
XLA Ops:
  7.2 0.0 all-gather.2.cloned.1.call-start
  7.2 0.7 multiply_exponential_fusion
  7.9 0.1 copy.10
  8.0 0.2 mul.55
  8.2 1.9 fusion.2
  10.1 0.0 all-gather.2.cloned.1.call-update
  10.1 0.0 all-reduce.4.cloned.1.call-start
  10.1 0.8 exponential_convert_fusion
  10.9 0.1 copy.9
  11.0 134.0 %all-gather.2.cloned.1.call-done = bf16[2048,2048]{1,0:T(8,128)(2,1)} async-done(((bf16[64,2048]{1,0:T(8,128)(2,1)}), bf16[2048,2048]{1,0:T(8,128)(2,1)}) %all-gather.2.cloned.1.call-update) | async-done | bytes 8388624 | tf_op jit(solution)/shard_map/all_gather | solution.py:48
  145.0 2.2 mul.52
  147.2 10.5 %fusion = f32[512,2048]{1,0:T(8,128)} fusion(bf16[2048,2048]{1,0:T(8,128)(2,1)} %all-gather.2.cloned.1.call-done, bf16[512,2048]{1,0:T(8,128)(2,1)} %param.7, bf16[64,8,16,128]{3,2,1,0:T(8,128)(2,1)S(1)} %bitcast.15), kind=kOutput, calls=%fused_computation.4 | convolution fusion | flops 4296015872 | bytes 16777216 | tf_op jit(solution)/shard_map/tf,qf->tq/dot_general | solution.py:52
  157.8 0.0 all-reduce.4.cloned.1.call-update
  157.8 1.3 dynamic-slice
  159.7 0.0 copy-done.1
  159.7 0.3 dynamic-update-slice
  160.0 16.6 %all-reduce = s32[2048]{0:T(1024)S(1)} all-reduce(s32[2048]{0:T(1024)S(1)} %dynamic-update-slice), channel_id=1, replica_groups=mesh['row'=32,'col'=16] {'row'}, use_global_device_ids=true, to_apply=%add | all-reduce | flops 2048 | bytes 16384
  176.6 2.4 multiply_reduce_fusion.1
  179.1 5.1 %multiply_reduce_fusion = f32[2048]{0:T(1024)S(1)} fusion(bf16[2048,2048]{1,0:T(8,128)(2,1)} %all-gather.2.cloned.1.call-done), kind=kLoop, calls=%fused_computation | loop fusion | flops 12580864 | bytes 8396800 | tf_op jit(solution)/shard_map/reduce_sum | solution.py:34
  184.1 85.9 %all-reduce.1 = (f32[2048]{0:T(1024)S(1)}, f32[512]{0:T(512)S(1)}) all-reduce(f32[2048]{0:T(1024)S(1)} %multiply_reduce_fusion, f32[512]{0:T(512)S(1)} %multiply_reduce_fusion.1), channel_id=1, replica_groups=mesh['row'=32,'col'=16] {'col'}, use_global_device_ids=true, to_apply=%region_4.0 | all-reduce | flops 2560 | bytes 20480 | tf_op jit(solution)/shard_map/psum | solution.py:51
  270.0 66.8 %all-reduce.4.cloned.1.call-done = f32[512,2048]{1,0:T(8,128)} async-done(((f32[512,2048]{1,0:T(8,128)}), f32[512,2048]{1,0:T(8,128)}) %all-reduce.4.cloned.1.call-update) | async-done | bytes 4194320 | tf_op jit(solution)/shard_map/psum | solution.py:55
  336.8 0.0 copy-done
  336.8 3.9 %fusion.3 = (f32[512]{0:T(512)}, f32[512,2048]{1,0:T(8,128)S(1)}) fusion(f32[2048]{0:T(1024)S(1)} %broadcast_add_fusion, f32[512]{0:T(512)S(1)} %broadcast_add_fusion.1, f32[512,2048]{1,0:T(8,128)} %all-reduce.4.cloned.1.call-done, s32[2048]{0:T(1024)S(1)} %all-reduce, s32[512]{0:T(512)S(1)} %copy-done), kind=kLoop, calls=%fused_computation.13 | loop fusion | flops 6290944 | bytes 8411136 | tf_op jit(solution)/shard_map/reduce_max | solution.py:57
  340.7 0.7 constant_dynamic-slice_fusion
  (5 shorter events, 0.0 us)
Async XLA Ops:
  7.2 137.9 %all-gather.2.cloned.1.call-start = ((), (), s32[]{:S(2)}) async-start(), calls=%async_computation | async-start | bytes 8650752 | tf_op jit(solution)/shard_map/all_gather | solution.py:48
  10.1 326.7 %all-reduce.4.cloned.1.call-start = ((), (), s32[]{:S(2)}) async-start(), calls=%async_computation.1 | async-start | bytes 8388608 | tf_op jit(solution)/shard_map/psum | solution.py:55
  157.8 2.0 copy-start.1
  179.1 157.8 %copy-start = (s32[512]{0:T(512)S(1)}, s32[512]{0:T(512)}, u32[]{:S(2)}) copy-start(s32[512]{0:T(512)} %param.9) | copy-start | bytes 6148
Sparse Core Ops, SparseCore 0:
  10.7 134.3 all-gather.1
  157.9 178.8 all-reduce.3
where the time goes:
time: 349 us; the launch traced here: 348 us
  waiting for transfers between devices  201 us (58%)
  blocking collectives  102 us (29%)
  other arithmetic  14.7 us (4%)
  between operations  14.7 us (4%)
  matrix products  10.5 us (3%)
  local copies, waits for them, and re-layouts  4.92 us (1%)
    all_gather x1, waiting for transfers between devices, shards(): lax.all_gather(query_pre, 'row', axis=0, tiled=True)  134 us
    psum x1, blocking collectives, shards(): train_sq, query_sq = lax.psum((train_part, squares(gathered)), 'col')  85.9 us
    psum x1, waiting for transfers between devices, shards(): raw = lax.psum(raw_part, 'col')  66.8 us
    unnamed x1, blocking collectives  16.6 us
    dot_general x1, matrix products, shards(): jnp.einsum('tf,qf->tq', train_grad, gathered, preferred_element_type=jnp....  10.5 us
    reduce_sum x2, other arithmetic, squares(): return jnp.sum(jnp.square(values.astype(jnp.float32)), axis=1)  7.5 us
  transfers between devices with their start and end apart: 2, of which 2 were waited for; matrix products, arithmetic and copies ran while one was open for 3% of the time, Pallas kernels for 0%

commit v1 on v0

v1 whole, which is shorter than its diff:
```python
import functools
import math

import jax
import jax.numpy as jnp
from jax import lax
from jax.experimental import pallas as pl
from jax.experimental.pallas import tpu as pltpu
from jax.sharding import PartitionSpec as P

P_SIZE = 32768
EPS = 1e-06
MESH = pl.DeviceIdType.MESH
F32 = jnp.float32
BF16 = jnp.bfloat16

NZ = 16
BLK = 64
KD = 2048
ROWS = 512
LANES = 128
NBLK = KD // LANES
NCH = 4
CH = BLK // NCH
XCH = 64
NX = ROWS // XCH


def dist(a, b):
    return jnp.minimum((a - b + NZ) % NZ, (b - a + NZ) % NZ)


def slot_of(z, block):
    first = (block // 2) * 2
    last = jnp.maximum(dist(z, first), dist(z, first + 1))
    return (last - 1) * 2 + block % 2


def pair_of(z, step):
    odd = (z + step) % 2
    return jnp.where(odd == 1, ((z + step) % NZ) // 2, ((z - step + NZ) % NZ) // 2)


def power(exps):
    return lax.shift_left(jnp.int32(1), exps + 3).astype(F32) * 0.125


def rcopy(src, dst, send, recv, device):
    return pltpu.make_async_remote_copy(
        src_ref=src, dst_ref=dst, send_sem=send, recv_sem=recv, device_id=device, device_id_type=MESH
    )


def kernel(
    tc_hbm, te_hbm, tid_ref, qc_hbm, qe_ref, qid_ref, pre_ref,
    cos_ref, peak_ref,
    tcode, texp, qcode, a_all, b_all, tsq, s1, r1, loc, s2, r2, acc, sx, rx, keep,
    mine, parts, meta, metas, tinv, tidb, ppart, peaks,
    in_sem, z_send, z_recv, x_send, x_recv, s1_send, s1_recv, s2_send, s2_recv,
    s3_send, s3_recv, a_send, a_recv, m_send, m_recv, p_send, p_recv,
):
    r, c = lax.axis_index("row"), lax.axis_index("col")
    xlo, z = r // NZ, r % NZ
    xhi, y, core = c // 8, (c // 2) % 4, c % 2
    up = (xlo * NZ + (z + 1) % NZ, c)
    down = (xlo * NZ + (z + NZ - 1) % NZ, c)
    xpair = ((1 - xlo) * NZ + z, c)
    xhop = (r, (c + 8) % 16)
    diag = ((1 - xlo) * NZ + z, (c + 8) % 16)
    twin = (r, c + 1 - 2 * core)
    home = xhi == xlo

    barrier = pltpu.get_barrier_semaphore()
    for peer in (up, down, xpair, diag):
        pl.semaphore_signal(barrier, inc=1, device_id=peer, device_id_type=MESH)

    def greet(k, _):
        pl.semaphore_signal(barrier, inc=1, device_id=(r, (c + k) % 16), device_id_type=MESH)
        return 0

    lax.fori_loop(1, 16, greet, 0)
    is_self = [jnp.logical_and(2 * c + i == r, r // 2 == c) for i in range(2)]
    for i in range(2):
        @pl.when(jnp.logical_not(is_self[i]))
        def _():
            pl.semaphore_signal(barrier, inc=1, device_id=(2 * c + i, r // 2), device_id_type=MESH)

    q_in = pltpu.make_async_copy(qc_hbm, qcode, in_sem.at[NX])
    q_in.start()
    e_in = pltpu.make_async_copy(te_hbm, texp, in_sem.at[NX + 1])
    e_in.start()

    def t_in(i):
        rows = pl.ds(i * XCH, XCH)
        return pltpu.make_async_copy(tc_hbm.at[rows], tcode.at[rows], in_sem.at[i])

    for i in range(NX):
        t_in(i).start()

    q_in.wait()
    own = slot_of(z, z) * BLK
    q_factor = power(qe_ref[...])
    qsq = jnp.zeros((BLK, LANES), F32)
    for j in range(NBLK):
        cols = pl.ds(j * LANES, LANES)
        value = (qcode[:, cols].astype(F32) * q_factor[:, j : j + 1] * pre_ref[j : j + 1, :]).astype(BF16)
        b_all[pl.ds(pl.multiple_of(own, BLK), BLK), cols] = value
        qsq += jnp.square(value.astype(F32))

    pl.semaphore_wait(
        barrier, 4 + 15 + 2 - is_self[0].astype(jnp.int32) - is_self[1].astype(jnp.int32)
    )

    def z_rows(zd, block, k):
        return pl.ds(pl.multiple_of(slot_of(zd, block) * BLK + k * CH, CH), CH)

    def z_copy(way, step, k):
        if way == 0:
            block, to, zd = (z - (step - 1) + NZ) % NZ, up, (z + 1) % NZ
        else:
            block, to, zd = (z + (step - 1)) % NZ, down, (z + NZ - 1) % NZ
        return rcopy(
            b_all.at[z_rows(z, block, k)], b_all.at[z_rows(zd, block, k)],
            z_send.at[way, step, k], z_recv.at[way, step, k], to,
        )

    def z_arrival(way, step, k):
        block = (z - step + NZ) % NZ if way == 0 else (z + step) % NZ
        rows = b_all.at[z_rows(z, block, k)]
        return rcopy(rows, rows, z_send.at[way, step, k], z_recv.at[way, step, k], up)

    def chunk_of(way, k):
        return k if way == 0 else (k + NCH // 2) % NCH

    for k in range(NCH):
        for way in range(2):
            z_copy(way, 1, chunk_of(way, k)).start()

    def x_copy(i):
        rows = pl.ds(pl.multiple_of(i * XCH, XCH), XCH)
        there = pl.ds(pl.multiple_of(ROWS + i * XCH, XCH), XCH)
        return rcopy(a_all.at[rows], a_all.at[there], x_send.at[i], x_recv.at[i], xpair)

    e_in.wait()

    def scale(i, _):
        t_in(i).wait()
        rows = pl.ds(pl.multiple_of(i * XCH, XCH), XCH)
        factor = power(texp[rows, :])
        total = jnp.zeros((XCH, LANES), F32)
        for j in range(NBLK):
            cols = pl.ds(j * LANES, LANES)
            value = tcode[rows, cols].astype(F32) * factor[:, j : j + 1]
            a_all[rows, cols] = value.astype(BF16)
            total += jnp.square(value)
        tsq[rows, :] = total

        @pl.when(i < 3)
        def _():
            x_copy(i).start()

        return 0

    lax.fori_loop(0, NX, scale, 0)

    mine[...] = jnp.zeros_like(mine)
    for g in range(4):
        mine[g : g + 1, :] = jnp.sum(tsq[pl.ds(g * LANES, LANES), :].T, axis=0, keepdims=True)
    wide = jnp.concatenate([qsq, jnp.zeros_like(qsq)], axis=0)
    mine[4:5, :] = jnp.sum(wide.T, axis=0, keepdims=True)

    def to_col(src, dst, send, recv, k):
        return rcopy(src, dst.at[c], send.at[k], recv.at[c], (r, (c + k) % 16))

    def from_col(src, dst, send, recv, k):
        who = (c + k) % 16
        return rcopy(src, dst.at[who], send.at[k], recv.at[who], (r, who))

    def send_parts(k, _):
        to_col(mine, parts, a_send, a_recv, k).start()
        return 0

    lax.fori_loop(1, 16, send_parts, 0)
    parts[c] = mine[...]

    def meta_copy(i):
        return rcopy(meta, metas.at[r % 2], m_send.at[i], m_recv.at[r % 2], (2 * c + i, r // 2))

    def norms():
        def got(k, _):
            from_col(mine, parts, a_send, a_recv, k).wait_recv()
            return 0

        lax.fori_loop(1, 16, got, 0)
        total = parts[0]
        for k in range(1, 16):
            total += parts[k]
        scaled = math.sqrt(P_SIZE) / jnp.sqrt(total + EPS)
        ids = tid_ref[...].astype(F32)
        for g in range(4):
            rows = pl.ds(g * LANES, LANES)
            tinv[rows, :] = jnp.broadcast_to(scaled[g : g + 1, :], (LANES, LANES)).T
            tidb[rows, :] = jnp.broadcast_to(ids[g : g + 1, :], (LANES, LANES)).T
        meta[...] = jnp.zeros_like(meta)
        meta[0:1, :] = total[4:5, :]
        meta[1:2, 0:BLK] = qid_ref[...].astype(F32)
        for i in range(2):
            @pl.when(is_self[i])
            def _():
                metas[i] = meta[...]

            @pl.when(jnp.logical_not(is_self[i]))
            def _():
                meta_copy(i).start()

    def big(q):
        return pl.ds(q * 256, 256)

    def small(q):
        return pl.ds(pl.multiple_of(q * LANES + 256, LANES), LANES)

    def hand(value, rows, q, step):
        j = pair_of(z, step)
        cd, yd = j % 2, j // 2

        @pl.when(core != cd)
        def _():
            s1[yd, rows, :] = value
            s1_copy(yd, rows, q).start()

        @pl.when(core == cd)
        def _():
            loc[yd, rows, :] = value

    def s1_copy(yd, rows, q):
        return rcopy(s1.at[yd, rows], r1.at[yd, rows], s1_send.at[yd, q], s1_recv.at[yd, q], twin)

    def s2_copy(yd, rows, q):
        k = (y - yd + 4) % 4 - 1
        return rcopy(
            s2.at[yd, rows], r2.at[k, rows], s2_send.at[yd, q], s2_recv.at[k, q], (r, xhi * 8 + yd * 2 + core)
        )

    def relay(rows, q, step):
        j = pair_of(z, step)
        cd, yd = j % 2, j // 2

        @pl.when(core == cd)
        def _():
            s1_copy(yd, rows, q).wait_recv()
            total = loc[yd, rows, :] + r1[yd, rows, :]

            @pl.when(y == yd)
            def _():
                acc[rows, :] = total

            @pl.when(y != yd)
            def _():
                s2[yd, rows, :] = total.astype(BF16)
                s2_copy(yd, rows, q).start()

    def dot(rows, cols):
        return lax.dot_general(
            a_all[rows, :], b_all[cols, :], (((1,), (1,)), ((), ())), preferred_element_type=F32
        )

    def q_at(step):
        return pl.ds(pl.multiple_of((step - 1) * LANES, LANES), LANES)

    def work_own(step, q):
        hand(dot(big(q), q_at(step)), big(q), q, step)

    def work_old(step):
        def one(q, _):
            hand(dot(small(q), q_at(step)), small(q), q, step)
            return 0

        lax.fori_loop(2, 2 + (step - 1) // 2, one, 0)

    def work_new(step):
        @pl.when(step % 2 == 0)
        def _():
            q = 1 + step // 2
            for i in (step - 2, step - 1):
                x_copy(i).wait_recv()

            def two(t, _):
                cols = pl.ds(pl.multiple_of(t * 2 * LANES, 2 * LANES), 2 * LANES)
                value = dot(small(q), cols)
                hand(value[:, :LANES], small(q), q, 2 * t + 1)
                hand(value[:, LANES:], small(q), q, 2 * t + 2)
                return 0

            lax.fori_loop(0, step // 2, two, 0)

    def pass_on(step):
        for q in range(2):
            relay(big(q), q, step)

        def one(q, _):
            relay(small(q), q, step)
            return 0

        lax.fori_loop(2, 2 + (step - 1) // 2, one, 0)

        @pl.when(step % 2 == 0)
        def _():
            q = 1 + step // 2

            def each(t, _):
                relay(small(q), q, t)
                return 0

            lax.fori_loop(1, step + 1, each, 0)

    def arrive(step, k):
        for way in range(2):
            chunk = chunk_of(way, k)

            @pl.when(jnp.logical_or(step < NZ // 2, k < NCH // 2))
            def _():
                z_arrival(way, step, chunk).wait_recv()

            @pl.when(jnp.logical_or(step < NZ // 2 - 1, jnp.logical_and(step == NZ // 2 - 1, k < NCH // 2)))
            def _():
                z_copy(way, step + 1, chunk).start()

    def body(step, _):
        for k in range(NCH):
            arrive(step, k)
            if k == 0:
                @pl.when(step + 2 < NX)
                def _():
                    x_copy(step + 2).start()

                @pl.when(step == 2)
                def _():
                    norms()

            @pl.when(step > 1)
            def _():
                if k < 2:
                    work_own(step - 1, k)
                elif k == 2:
                    work_old(step - 1)
                else:
                    work_new(step - 1)

        @pl.when(step > 2)
        def _():
            pass_on(step - 2)

        return 0

    lax.fori_loop(1, NZ // 2 + 1, body, 0)
    last = NZ // 2
    pass_on(last - 1)
    for q in range(2):
        work_own(last, q)
    work_old(last)
    work_new(last)
    pass_on(last)

    def summed(rows, q):
        total = acc[rows, :]
        for k in range(3):
            rcopy(r2.at[k, rows], r2.at[k, rows], s2_send.at[0, q], s2_recv.at[k, q], twin).wait_recv()
            total += r2[k, rows, :].astype(F32)
        return total

    def s3_own(u):
        rows = pl.ds(u * LANES, LANES)
        return rcopy(sx.at[rows], rx.at[0, rows], s3_send.at[u], s3_recv.at[0, u], xhop)

    def s3_pair(u):
        rows, there = pl.ds(ROWS + u * LANES, LANES), pl.ds(u * LANES, LANES)
        return rcopy(sx.at[rows], rx.at[0, there], s3_send.at[4 + u], s3_recv.at[0, u], xpair)

    def s3_diag(u):
        rows, there = pl.ds(ROWS + u * LANES, LANES), pl.ds(u * LANES, LANES)
        return rcopy(sx.at[rows], rx.at[1, there], s3_send.at[4 + u], s3_recv.at[1, u], diag)

    for q in range(2):
        total = summed(big(q), q)

        @pl.when(home)
        def _():
            keep[big(q), :] = total

        @pl.when(jnp.logical_not(home))
        def _():
            sx[big(q), :] = total.astype(BF16)
            s3_own(2 * q).start()
            s3_own(2 * q + 1).start()

    for u in range(4):
        sx[pl.ds(ROWS + u * LANES, LANES), :] = summed(pl.ds(ROWS + u * LANES, LANES), u + 2).astype(BF16)

        @pl.when(home)
        def _():
            s3_pair(u).start()

        @pl.when(jnp.logical_not(home))
        def _():
            s3_diag(u).start()

    for i in range(2):
        @pl.when(jnp.logical_not(is_self[i]))
        def _():
            rcopy(meta, metas.at[i], m_send.at[i], m_recv.at[i], up).wait_recv()

    lane = lax.broadcasted_iota(jnp.int32, (8, LANES), 1)
    both = jnp.where(lane < BLK, metas[0], pltpu.roll(metas[1], BLK, 1))
    q_inv = 1.0 / jnp.sqrt(both[0:1, :] + EPS)
    q_ids = both[1:2, :]

    ppart[...] = jnp.zeros_like(ppart)
    for u in range(4):
        rows = pl.ds(u * LANES, LANES)

        s3_pair(u).wait_recv()

        @pl.when(jnp.logical_not(home))
        def _():
            s3_diag(u).wait_recv()
            keep[rows, :] = rx[1, rows, :].astype(F32)

        raw = keep[rows, :] + rx[0, rows, :].astype(F32)
        value = raw * tinv[rows, :] * q_inv
        value = jnp.where(tidb[rows, :] == q_ids, 0.0, value)
        cos_ref[rows, :] = value
        ppart[u : u + 1, :] = jnp.max(value.T, axis=0, keepdims=True)

    def send_peaks(k, _):
        to_col(ppart, peaks, p_send, p_recv, k).start()
        return 0

    lax.fori_loop(1, 16, send_peaks, 0)
    peaks[c] = ppart[...]

    def sent(step, _):
        for k in range(NCH):
            for way in range(2):
                z_copy(way, step, k).wait_send()
        return 0

    lax.fori_loop(1, NZ // 2, sent, 0)
    for k in range(NCH // 2):
        for way in range(2):
            z_copy(way, NZ // 2, chunk_of(way, k)).wait_send()

    def x_sent(i, _):
        x_copy(i).wait_send()
        return 0

    lax.fori_loop(0, NX, x_sent, 0)

    def s_sent(yd, _):
        for q in range(2):
            s1_copy(yd, big(q), q).wait_send()

            @pl.when(yd != y)
            def _():
                s2_copy(yd, big(q), q).wait_send()

        for q in range(2, 6):
            s1_copy(yd, small(q), q).wait_send()

            @pl.when(yd != y)
            def _():
                s2_copy(yd, small(q), q).wait_send()

        return 0

    lax.fori_loop(0, 4, s_sent, 0)
    for u in range(4):
        @pl.when(jnp.logical_not(home))
        def _():
            s3_own(u).wait_send()

        s3_pair(u).wait_send()

    for i in range(2):
        @pl.when(jnp.logical_not(is_self[i]))
        def _():
            meta_copy(i).wait_send()

    def col_done(k, _):
        to_col(mine, parts, a_send, a_recv, k).wait_send()
        to_col(ppart, peaks, p_send, p_recv, k).wait_send()
        from_col(ppart, peaks, p_send, p_recv, k).wait_recv()
        return 0

    lax.fori_loop(1, 16, col_done, 0)
    best = peaks[0]
    for k in range(1, 16):
        best = jnp.maximum(best, peaks[k])
    peak_ref[...] = best[0:4, :]


def shards(train_codes, train_exps, train_ids, query_codes, query_exps, query_ids, precond):
    dma = pltpu.SemaphoreType.DMA
    vmem = pl.BlockSpec(memory_space=pltpu.VMEM)
    hbm = pl.BlockSpec(memory_space=pl.ANY)
    cosines, peak = pl.pallas_call(
        kernel,
        out_shape=(jax.ShapeDtypeStruct((ROWS, LANES), F32), jax.ShapeDtypeStruct((4, LANES), F32)),
        in_specs=[hbm, hbm, vmem, hbm, vmem, vmem, vmem],
        out_specs=(vmem, vmem),
        scratch_shapes=[
            pltpu.VMEM((ROWS, KD), BF16),
            pltpu.VMEM((ROWS, NBLK), jnp.int32),
            pltpu.VMEM((BLK, KD), BF16),
            pltpu.VMEM((2 * ROWS, KD), BF16),
            pltpu.VMEM((NZ * BLK, KD), BF16),
            pltpu.VMEM((ROWS, LANES), F32),
            pltpu.VMEM((4, 2 * ROWS, LANES), F32),
            pltpu.VMEM((4, 2 * ROWS, LANES), F32),
            pltpu.VMEM((4, 2 * ROWS, LANES), F32),
            pltpu.VMEM((4, 2 * ROWS, LANES), BF16),
            pltpu.VMEM((3, 2 * ROWS, LANES), BF16),
            pltpu.VMEM((2 * ROWS, LANES), F32),
            pltpu.VMEM((2 * ROWS, LANES), BF16),
            pltpu.VMEM((2, ROWS, LANES), BF16),
            pltpu.VMEM((ROWS, LANES), F32),
            pltpu.VMEM((8, LANES), F32),
            pltpu.VMEM((16, 8, LANES), F32),
            pltpu.VMEM((8, LANES), F32),
            pltpu.VMEM((2, 8, LANES), F32),
            pltpu.VMEM((ROWS, LANES), F32),
            pltpu.VMEM((ROWS, LANES), F32),
            pltpu.VMEM((8, LANES), F32),
            pltpu.VMEM((16, 8, LANES), F32),
            dma((NX + 2,)),
            dma((2, NZ // 2 + 1, NCH)), dma((2, NZ // 2 + 1, NCH)),
            dma((NX,)), dma((NX,)),
            dma((4, 6)), dma((4, 6)),
            dma((4, 6)), dma((3, 6)),
            dma((8,)), dma((2, 4)),
            dma((16,)), dma((16,)),
            dma((2,)), dma((2,)),
            dma((16,)), dma((16,)),
        ],
        compiler_params=pltpu.CompilerParams(
            collective_id=0, has_side_effects=True, vmem_limit_bytes=48 * 2**20
        ),
        cost_estimate=pl.CostEstimate(
            flops=2 * ROWS * 2048 * KD, bytes_accessed=3 * 2**20, transcendentals=0
        ),
    )(
        train_codes, train_exps, train_ids.reshape(4, LANES), query_codes, query_exps,
        query_ids.reshape(1, BLK), precond.reshape(NBLK, LANES),
    )
    return cosines, peak.reshape(ROWS)


def solution(mesh):
    in_specs = (
        P("row", "col"),
        P("row", "col"),
        P("row"),
        P("row", "col"),
        P("row", "col"),
        P("row"),
        P("col"),
    )
    out_specs = (P("row", "col"), P("row"))
    return jax.shard_map(shards, mesh=mesh, in_specs=in_specs, out_specs=out_specs, check_vma=False)
```

time: 349 us -> 107 us (0.31)
  waiting for transfers between devices: 201 us -> 0 us
  blocking collectives: 102 us -> 0 us
  Pallas kernels: 0 us -> 98.7 us
  other arithmetic: 14.7 us -> 0 us
  between operations: 14.7 us -> 0.66 us
  matrix products: 10.5 us -> 0 us
    all_gather x1 -> x0, waiting for transfers between devices: 134 us -> none  [shards(): lax.all_gather(query_pre, 'row', axis=0, tiled=True)]
    pallas_call x0 -> x1, Pallas kernels: none -> 98.7 us  [shards(): pl.pallas_call(kernel, out_shape=(jax.ShapeDtypeStruct((ROWS, LANES), F32...]
    psum x1 -> x0, blocking collectives: 85.9 us -> none  [shards(): train_sq, query_sq = lax.psum((train_part, squares(gathered)), 'col')]
    psum x1 -> x0, waiting for transfers between devices: 66.8 us -> none  [shards(): raw = lax.psum(raw_part, 'col')]
    unnamed x1 -> x0, blocking collectives: 16.6 us -> none
    dot_general x1 -> x0, matrix products: 10.5 us -> none  [shards(): jnp.einsum('tf,qf->tq', train_grad, gathered, preferred_element_type=jnp....]
    reduce_sum x2 -> x0, other arithmetic: 7.5 us -> none  [squares(): return jnp.sum(jnp.square(values.astype(jnp.float32)), axis=1)]
    unnamed x7 -> x14, local copies, waits for them, and re-layouts: 1.56 us -> 7.51 us
  transfers between devices with their start and end apart: 2 -> 0, of which waited for: 2 -> 0; matrix products, arithmetic and copies ran while one was open for 3% -> 0% of each run, Pallas kernels for 0% -> 0%
where the time goes in v1:
time: 107 us
  Pallas kernels  98.7 us (92%)
  local copies, waits for them, and re-layouts  7.51 us (7%)
    pallas_call x1, Pallas kernels, shards(): pl.pallas_call(kernel, out_shape=(jax.ShapeDtypeStruct((ROWS, LANES), F32...  98.7 us
    unnamed x14, local copies, waits for them, and re-layouts  7.51 us

profile of v1, /device:TPU:1, one launch (start us, length us, event | category | flops | bytes accessed | tf_op | source)
XLA Modules:
  0.0 106.9 jit_solution(12498705342701280575)
XLA Ops:
  0.6 0.8 copy.10.qe_ref
  1.4 0.9 copy.9.te_hbm
  2.3 0.0 copy-start
  2.3 1.6 %copy-done = bf16[512,2048]{1,0:T(8,128)(2,1)S(1)} copy-done((bf16[512,2048]{1,0:T(8,128)(2,1)S(1)}, bf16[512,2048]{1,0:T(8,128)(2,1)}, u32[]{:S(2)}) %copy-start) | copy-done | bytes 2097176
  3.9 0.0 copy-start.1
  3.9 0.9 copy-done.1
  4.8 0.0 copy-start.2
  4.8 0.7 copy-done.2
  5.5 0.0 copy-start.3
  5.5 0.7 copy-done.3
  6.2 0.0 copy-start.4
  6.2 0.7 copy-done.4
  6.9 98.7 %shard_map.86 = (f32[512,128]{1,0:T(8,128)S(1)}, f32[4,128]{1,0:T(4,128)S(1)}) custom-call(bf16[512,2048]{1,0:T(8,128)(2,1)S(1)} %copy-done, s32[512,16]{1,0:T(8,128)S(1)} %copy.9.te_hbm, s32[4,128]{1,0:T(4,128)S(1)} %bitcast.6, bf16[64,2048]{1,0:T(8,128)(2,1)S(1)} %copy-done.1, s32[64,16]{1,0:T(8,128)S(1)} %copy.10.qe_ref, s32[1,64]{1,0:T(1,128)S(1)} %bitcast.7, ...), custom_call_target="tpu_custom_call" | custom-call | flops 4294967296 | bytes 3145728 | tf_op jit(solution)/shard_map/pallas_call | solution.py:505
  105.6 0.7 copy.13
  106.3 0.6 copy.14
Async XLA Ops:
  2.3 1.6 %copy-start = (bf16[512,2048]{1,0:T(8,128)(2,1)S(1)}, bf16[512,2048]{1,0:T(8,128)(2,1)}, u32[]{:S(2)}) copy-start(bf16[512,2048]{1,0:T(8,128)(2,1)} %tc_hbm.1) | copy-start | bytes 6291460
  3.9 0.9 copy-start.1
  4.8 0.7 copy-start.2
  5.5 0.7 copy-start.3
  6.2 0.7 copy-start.4

commit v2 on v1

v2 whole, which is shorter than its diff:
```python
import functools
import math

import jax
import jax.numpy as jnp
from jax import lax
from jax.experimental import pallas as pl
from jax.experimental.pallas import tpu as pltpu
from jax.sharding import PartitionSpec as P

P_SIZE = 32768
EPS = 1e-06
MESH = pl.DeviceIdType.MESH
F32 = jnp.float32
BF16 = jnp.bfloat16

NZ = 16
BLK = 64
KD = 2048
ROWS = 512
LANES = 128
NBLK = KD // LANES
NCH = 4
CH = BLK // NCH
XCH = 16
NX = ROWS // XCH
XLEAD = 4
NIN = 8
TCH = ROWS // NIN
VMEM = 62 * 2**20


def wrap(z):
    return lax.rem(z + NZ, NZ)


def pair_of(z, step):
    odd = lax.rem(z + step, 2)
    return lax.div(wrap(z - step + 2 * step * odd), 2)


def power(exps):
    return lax.shift_left(jnp.int32(1), exps + 3).astype(F32) * 0.125


def rcopy(src, dst, send, recv, device):
    return pltpu.make_async_remote_copy(
        src_ref=src, dst_ref=dst, send_sem=send, recv_sem=recv, device_id=device, device_id_type=MESH
    )


def kernel(
    tc_hbm, te_hbm, tid_hbm, qc_hbm, qe_hbm, qid_hbm, pre_hbm,
    cos_hbm, peak_ref,
    tcode, texp, tfac, tid_ref, qcode, qexp, qid_ref, pre_ref, a_all, b_all, tsq, prod, r1, s2, r2, acc, sx, rx, keep,
    mine, parts, meta, metas, tinv, ppart, peaks, cosv,
    in_sem, z_send, z_recv, x_send, x_recv, s1_send, s1_recv, s2_send, s2_recv, n1_send, n1_recv, n2_send, n2_recv,
    s3_send, s3_recv, a_send, a_recv, m_send, m_recv, p_send, p_recv,
):
    r, c = lax.axis_index("row"), lax.axis_index("col")
    xlo, z = lax.div(r, NZ), lax.rem(r, NZ)
    xhi, y, core = lax.div(c, 8), lax.rem(lax.div(c, 2), 4), lax.rem(c, 2)
    up = (xlo * NZ + wrap(z + 1), c)
    down = (xlo * NZ + wrap(z - 1), c)
    xpair = ((1 - xlo) * NZ + z, c)
    xhop = (r, lax.rem(c + 8, 16))
    diag = ((1 - xlo) * NZ + z, lax.rem(c + 8, 16))
    twin = (r, c + 1 - 2 * core)
    home = xhi == xlo

    barrier = pltpu.get_barrier_semaphore()
    for peer in (up, down, xpair, diag):
        pl.semaphore_signal(barrier, inc=1, device_id=peer, device_id_type=MESH)

    def greet(k, _):
        pl.semaphore_signal(barrier, inc=1, device_id=(r, lax.rem(c + k, 16)), device_id_type=MESH)
        return 0

    lax.fori_loop(1, 16, greet, 0)
    is_self = [jnp.logical_and(2 * c + i == r, lax.div(r, 2) == c) for i in range(2)]
    for i in range(2):
        @pl.when(jnp.logical_not(is_self[i]))
        def _():
            pl.semaphore_signal(barrier, inc=1, device_id=(2 * c + i, lax.div(r, 2)), device_id_type=MESH)

    first_in = [
        pltpu.make_async_copy(src, dst, in_sem.at[NIN + i])
        for i, (src, dst) in enumerate(
            [(qc_hbm, qcode), (qe_hbm, qexp), (pre_hbm, pre_ref), (te_hbm, texp), (tid_hbm, tid_ref), (qid_hbm, qid_ref)]
        )
    ]
    for copy in first_in:
        copy.start()

    def t_in(i):
        rows = pl.ds(i * TCH, TCH)
        return pltpu.make_async_copy(tc_hbm.at[rows], tcode.at[rows], in_sem.at[i])

    for i in range(NIN):
        t_in(i).start()

    for copy in first_in[:3]:
        copy.wait()
    mine_at = pl.multiple_of(z * BLK, BLK)
    q_factor = power(qexp[...]).T
    qsq = jnp.zeros((BLK, LANES), F32)
    for j in range(NBLK):
        cols = pl.ds(j * LANES, LANES)
        value = (qcode[:, cols].astype(F32) * q_factor[:, j : j + 1] * pre_ref[j : j + 1, :]).astype(BF16)
        b_all[pl.ds(mine_at, BLK), cols] = value
        qsq += jnp.square(value.astype(F32))

    pl.semaphore_wait(
        barrier, 4 + 15 + 2 - is_self[0].astype(jnp.int32) - is_self[1].astype(jnp.int32)
    )

    def z_rows(block, k):
        return pl.ds(pl.multiple_of(block * BLK + k * CH, CH), CH)

    def z_copy(way, step, k):
        block, to = (wrap(z - step + 1), up) if way == 0 else (wrap(z + step - 1), down)
        rows = b_all.at[z_rows(block, k)]
        return rcopy(rows, rows, z_send.at[way, step, k], z_recv.at[way, step, k], to)

    def z_arrival(way, step, k):
        block = wrap(z - step) if way == 0 else wrap(z + step)
        rows = b_all.at[z_rows(block, k)]
        return rcopy(rows, rows, z_send.at[way, step, k], z_recv.at[way, step, k], up)

    def chunk_of(way, k):
        return k if way == 0 else (k + NCH // 2) % NCH

    for k in range(NCH):
        for way in range(2):
            z_copy(way, 1, chunk_of(way, k)).start()

    def x_copy(i):
        rows = pl.ds(pl.multiple_of(i * XCH, XCH), XCH)
        there = pl.ds(pl.multiple_of(ROWS + i * XCH, XCH), XCH)
        g = lax.div(i, LANES // XCH)
        return rcopy(a_all.at[rows], a_all.at[there], x_send.at[g], x_recv.at[g], xpair)

    def x_group(g):
        rows = pl.ds(pl.multiple_of(g * LANES, LANES), LANES)
        there = pl.ds(pl.multiple_of(ROWS + g * LANES, LANES), LANES)
        return rcopy(a_all.at[rows], a_all.at[there], x_send.at[g], x_recv.at[g], xpair)

    for copy in first_in[3:]:
        copy.wait()
    tfac[...] = power(texp[...]).T

    def scale(i, _):
        t_in(i).wait()
        rows = pl.ds(pl.multiple_of(i * TCH, TCH), TCH)
        factor = tfac[rows, :]
        total = jnp.zeros((TCH, LANES), F32)
        for j in range(NBLK):
            cols = pl.ds(j * LANES, LANES)
            value = tcode[rows, cols].astype(F32) * factor[:, j : j + 1]
            a_all[rows, cols] = value.astype(BF16)
            total += jnp.square(value)
        tsq[rows, :] = total

        @pl.when(i < 2)
        def _():
            for k in range(XLEAD // 2):
                x_copy(i * (XLEAD // 2) + k).start()

        return 0

    lax.fori_loop(0, NIN, scale, 0)

    mine[...] = jnp.zeros_like(mine)
    for g in range(4):
        mine[g : g + 1, :] = jnp.sum(tsq[pl.ds(g * LANES, LANES), :].T, axis=0, keepdims=True)
    wide = jnp.concatenate([qsq, jnp.zeros_like(qsq)], axis=0)
    mine[4:5, :] = jnp.sum(wide.T, axis=0, keepdims=True)

    def to_col(src, dst, send, recv, k):
        return rcopy(src, dst.at[c], send.at[k], recv.at[c], (r, lax.rem(c + k, 16)))

    def from_col(src, dst, send, recv, k):
        who = lax.rem(c + k, 16)
        return rcopy(src, dst.at[who], send.at[k], recv.at[who], (r, who))

    def send_parts(k, _):
        to_col(mine, parts, a_send, a_recv, k).start()
        return 0

    lax.fori_loop(1, 16, send_parts, 0)
    parts[c] = mine[...]

    def meta_copy(i):
        return rcopy(meta, metas.at[lax.rem(r, 2)], m_send.at[i], m_recv.at[lax.rem(r, 2)], (2 * c + i, lax.div(r, 2)))

    def norms():
        def got(k, _):
            from_col(mine, parts, a_send, a_recv, k).wait_recv()
            return 0

        lax.fori_loop(1, 16, got, 0)
        total = parts[0]
        for k in range(1, 16):
            total += parts[k]
        tinv[...] = math.sqrt(P_SIZE) / jnp.sqrt(total + EPS)
        meta[...] = jnp.zeros_like(meta)
        meta[0:1, :] = total[4:5, :]
        meta[1:2, 0:BLK] = qid_ref[...].astype(F32)
        for i in range(2):
            @pl.when(is_self[i])
            def _():
                metas[i] = meta[...]

            @pl.when(jnp.logical_not(is_self[i]))
            def _():
                meta_copy(i).start()

    last = NZ // 2
    late = lax.rem(z, 2) * BLK
    soon = BLK - late

    def whole(lo, hi):
        return pl.ds(lo, hi - lo), pl.ds(0, LANES)

    def half(lo, hi, q0):
        return pl.ds(lo, hi - lo), pl.ds(pl.multiple_of(q0, BLK), BLK)

    def group(g):
        return pl.ds(g, 1), pl.ds(0, LANES)

    def pair_at(step):
        j = pair_of(z, step)
        return lax.div(j, 2), lax.rem(j, 2)

    def s1_copy(yd, part, i):
        w, q = part
        return rcopy(
            prod.at[yd, 1 - core, w, q], r1.at[yd, w, q], s1_send.at[yd, i], s1_recv.at[yd, i], twin
        )

    def s2_copy(yd, part, i):
        w, q = part
        k = lax.rem(y - yd + 4, 4) - 1
        return rcopy(
            s2.at[yd, w, q], r2.at[k, w, q], s2_send.at[yd, i], s2_recv.at[k, i], (r, xhi * 8 + yd * 2 + core)
        )

    def s2_arrival(k, part, i):
        w, q = part
        return rcopy(r2.at[k, w, q], r2.at[k, w, q], s2_send.at[0, i], s2_recv.at[k, i], twin)

    def dot(step, part):
        w, q = part
        yd, cd = pair_at(step)
        queries = pl.ds(pl.multiple_of((2 * yd + cd) * LANES + q.start, BLK), q.size)
        rows = pl.ds(pl.multiple_of(w.start * LANES, LANES), w.size * LANES)
        value = lax.dot_general(
            b_all[queries, :], a_all[rows, :], (((1,), (1,)), ((), ())), preferred_element_type=F32
        )
        for n in range(w.size):
            prod[yd, cd, w.start + n, q, :] = value[:, n * LANES : (n + 1) * LANES]

    def work(step, part, i):
        yd, cd = pair_at(step)
        dot(step, part)

        @pl.when(core != cd)
        def _():
            s1_copy(yd, part, i).start()

    def relay(step, part, i):
        w, q = part
        yd, cd = pair_at(step)

        @pl.when(core == cd)
        def _():
            s1_copy(yd, part, i).wait_recv()

            @pl.when(y == yd)
            def _():
                acc[w, q, :] = prod[yd, cd, w, q, :] + r1[yd, w, q, :]

            @pl.when(y != yd)
            def _():
                s2[yd, w, q, :] = (prod[yd, cd, w, q, :] + r1[yd, w, q, :]).astype(BF16)
                s2_copy(yd, part, i).start()

    def old(step, what):
        def one(g, _):
            what(step, group(4 + g), 2 + g)
            return 0

        lax.fori_loop(0, lax.div(step - 1, 2), one, 0)

    def new(step, what):
        @pl.when(jnp.logical_and(lax.rem(step, 2) == 0, step > 0))
        def _():
            g = lax.div(step, 2) - 1
            if what is work:
                x_group(g).wait_recv()

            def each(t, _):
                what(t, group(4 + g), 2 + g)
                return 0

            lax.fori_loop(1, step + 1, each, 0)

    def newest_copy():
        return rcopy(prod.at[:, 1 - core, 7], r1.at[:, 7], n1_send, n1_recv, twin)

    def newest_on(n):
        yd = lax.rem(y + n, 4)
        return rcopy(
            s2.at[yd, 7], r2.at[3 - n, 7], n2_send.at[n - 1], n2_recv.at[3 - n], (r, xhi * 8 + yd * 2 + core)
        )

    def work_newest():
        x_group(3).wait_recv()
        value = lax.dot_general(
            b_all[...], a_all[pl.ds(7 * LANES, LANES), :], (((1,), (1,)), ((), ())), preferred_element_type=F32
        )
        for j in range(8):
            prod[j // 2, j % 2, 7] = value[j * LANES : (j + 1) * LANES, :]
        newest_copy().start()

    def relay_newest():
        newest_copy().wait_recv()
        for n in (1, 2, 3):
            yd = lax.rem(y + n, 4)
            s2[yd, 7] = (prod[yd, core, 7] + r1[yd, 7]).astype(BF16)
            newest_on(n).start()
        acc[7] = prod[y, core, 7] + r1[y, 7]

    def arrive(step, k):
        for way in range(2):
            chunk = chunk_of(way, k)

            @pl.when(jnp.logical_or(step < NZ // 2, k < NCH // 2))
            def _():
                z_arrival(way, step, chunk).wait_recv()

            @pl.when(jnp.logical_or(step < NZ // 2 - 1, jnp.logical_and(step == NZ // 2 - 1, k < NCH // 2)))
            def _():
                z_copy(way, step + 1, chunk).start()

    def follow(step, k):
        i = (step - 1) * NCH + k + XLEAD

        @pl.when(i < NX)
        def _():
            x_copy(i).start()

    own = whole(0, 4)

    def body(step, _):
        arrive(step, 0)
        follow(step, 0)

        @pl.when(step > 1)
        def _():
            old(step - 1, work)
            relay(step - 1, own, 0)

        arrive(step, 1)
        follow(step, 1)
        new(step - 1, work)
        arrive(step, 2)
        follow(step, 2)

        @pl.when(step > 1)
        def _():
            old(step - 1, relay)

        new(step - 1, relay)

        @pl.when(step == 2)
        def _():
            norms()

        arrive(step, 3)
        follow(step, 3)
        work(step, own, 0)
        return 0

    lax.fori_loop(1, last, body, 0)
    arrive(last, 0)
    old(last - 1, work)
    relay(last - 1, own, 0)
    work(last, half(0, 4, soon), 0)
    arrive(last, 1)
    work(last, half(0, 4, late), 1)
    old(last - 1, relay)
    relay(last, half(0, 4, soon), 0)
    work(last, half(4, 7, soon), 2)
    relay(last, half(0, 4, late), 1)
    work(last, half(4, 7, late), 3)
    work_newest()
    relay(last, half(4, 7, soon), 2)
    relay(last, half(4, 7, late), 3)
    relay_newest()

    lyd, lcd = pair_at(last)
    is_last = jnp.logical_and(y == lyd, core == lcd)

    def y_arrived(parts_last, parts_else):
        @pl.when(is_last)
        def _():
            for k in range(3):
                for part, i in parts_last:
                    s2_arrival(k, part, i).wait_recv()

        @pl.when(jnp.logical_not(is_last))
        def _():
            for k in range(3):
                for part, i in parts_else:
                    s2_arrival(k, part, i).wait_recv()

    def summed(w):
        return acc[w] + r2[0, w].astype(F32) + r2[1, w].astype(F32) + r2[2, w].astype(F32)

    def s3_own(u):
        return rcopy(sx.at[u], rx.at[0, u], s3_send.at[u], s3_recv.at[0, u], xhop)

    def s3_pair(u):
        return rcopy(sx.at[4 + u], rx.at[0, u], s3_send.at[4 + u], s3_recv.at[0, u], xpair)

    def s3_diag(u):
        return rcopy(sx.at[4 + u], rx.at[1, u], s3_send.at[4 + u], s3_recv.at[1, u], diag)

    own_parts = ([(half(0, 4, soon), 0), (half(0, 4, late), 1)], [(own, 0)])
    old_parts = ([(half(4, 7, soon), 2), (half(4, 7, late), 3)], [(group(4 + g), 2 + g) for g in range(3)])
    y_arrived(*own_parts)
    for u in range(4):
        total = summed(u)

        @pl.when(home)
        def _():
            keep[u] = total

        @pl.when(jnp.logical_not(home))
        def _():
            sx[u] = total.astype(BF16)
            s3_own(u).start()

    for u in range(4):
        if u == 0:
            y_arrived(*old_parts)
        if u == 3:
            for n in (1, 2, 3):
                newest_on(n).wait_recv()
        sx[4 + u] = summed(4 + u).astype(BF16)

        @pl.when(home)
        def _():
            s3_pair(u).start()

        @pl.when(jnp.logical_not(home))
        def _():
            s3_diag(u).start()

    for i in range(2):
        @pl.when(jnp.logical_not(is_self[i]))
        def _():
            rcopy(meta, metas.at[i], m_send.at[i], m_recv.at[i], up).wait_recv()

    lane = lax.broadcasted_iota(jnp.int32, (8, LANES), 1)
    both = jnp.where(lane < BLK, metas[0], pltpu.roll(metas[1], BLK, 1))
    q_inv = jnp.broadcast_to(1.0 / jnp.sqrt(both[0:1, :] + EPS), (LANES, LANES)).T
    q_ids = jnp.broadcast_to(both[1:2, :], (LANES, LANES)).T
    t_ids = tid_ref[...].astype(F32)

    def out_copy(u):
        rows = pl.ds(u * LANES, LANES)
        return pltpu.make_async_copy(cosv.at[rows], cos_hbm.at[rows], in_sem.at[u])

    ppart[...] = jnp.zeros_like(ppart)
    for u in range(4):
        s3_pair(u).wait_recv()

        @pl.when(jnp.logical_not(home))
        def _():
            s3_diag(u).wait_recv()
            keep[u] = rx[1, u].astype(F32)

        raw = keep[u] + rx[0, u].astype(F32)
        value = raw * q_inv * tinv[u : u + 1, :]
        value = jnp.where(q_ids == t_ids[u : u + 1, :], 0.0, value)
        ppart[u : u + 1, :] = jnp.max(value, axis=0, keepdims=True)
        cosv[pl.ds(u * LANES, LANES), :] = value.T

    def send_peaks(k, _):
        to_col(ppart, peaks, p_send, p_recv, k).start()
        return 0

    lax.fori_loop(1, 16, send_peaks, 0)
    peaks[c] = ppart[...]
    for u in range(4):
        out_copy(u).start()

    def sent(step, _):
        for k in range(NCH):
            for way in range(2):
                z_copy(way, step, k).wait_send()
        return 0

    lax.fori_loop(1, NZ // 2, sent, 0)
    for k in range(NCH // 2):
        for way in range(2):
            z_copy(way, NZ // 2, chunk_of(way, k)).wait_send()

    def x_sent(i, _):
        x_group(i).wait_send()
        return 0

    lax.fori_loop(0, 4, x_sent, 0)

    def s_sent(yd, _):
        def out(copy, j):
            for of_last, some in ((True, own_parts[0] + old_parts[0]), (False, own_parts[1] + old_parts[1])):
                @pl.when((j == pair_of(z, last)) == of_last)
                def _():
                    for part, i in some:
                        copy(yd, part, i).wait_send()

        out(s1_copy, 2 * yd + 1 - core)

        @pl.when(yd != y)
        def _():
            out(s2_copy, 2 * yd + core)

        return 0

    lax.fori_loop(0, 4, s_sent, 0)
    newest_copy().wait_send()
    for n in (1, 2, 3):
        newest_on(n).wait_send()
    for u in range(4):
        @pl.when(jnp.logical_not(home))
        def _():
            s3_own(u).wait_send()

        s3_pair(u).wait_send()

    for i in range(2):
        @pl.when(jnp.logical_not(is_self[i]))
        def _():
            meta_copy(i).wait_send()

    def col_done(k, _):
        to_col(mine, parts, a_send, a_recv, k).wait_send()
        to_col(ppart, peaks, p_send, p_recv, k).wait_send()
        from_col(ppart, peaks, p_send, p_recv, k).wait_recv()
        return 0

    lax.fori_loop(1, 16, col_done, 0)
    best = peaks[0]
    for k in range(1, 16):
        best = jnp.maximum(best, peaks[k])
    peak_ref[...] = best[0:4, :]
    for u in range(4):
        out_copy(u).wait()


def shards(train_codes, train_exps, train_ids, query_codes, query_exps, query_ids, precond):
    dma = pltpu.SemaphoreType.DMA
    vmem = pl.BlockSpec(memory_space=pltpu.VMEM)
    hbm = pl.BlockSpec(memory_space=pl.ANY)
    cosines, peak = pl.pallas_call(
        kernel,
        out_shape=(jax.ShapeDtypeStruct((ROWS, LANES), F32), jax.ShapeDtypeStruct((4, LANES), F32)),
        in_specs=[hbm] * 7,
        out_specs=(hbm, vmem),
        scratch_shapes=[
            pltpu.VMEM((ROWS, KD), BF16),
            pltpu.VMEM((NBLK, ROWS), jnp.int32),
            pltpu.VMEM((ROWS, NBLK), F32),
            pltpu.VMEM((4, LANES), jnp.int32),
            pltpu.VMEM((BLK, KD), BF16),
            pltpu.VMEM((NBLK, BLK), jnp.int32),
            pltpu.VMEM((1, BLK), jnp.int32),
            pltpu.VMEM((NBLK, LANES), F32),
            pltpu.VMEM((2 * ROWS, KD), BF16),
            pltpu.VMEM((NZ * BLK, KD), BF16),
            pltpu.VMEM((ROWS, LANES), F32),
            pltpu.VMEM((4, 2, 8, LANES, LANES), F32),
            pltpu.VMEM((4, 8, LANES, LANES), F32),
            pltpu.VMEM((4, 8, LANES, LANES), BF16),
            pltpu.VMEM((3, 8, LANES, LANES), BF16),
            pltpu.VMEM((8, LANES, LANES), F32),
            pltpu.VMEM((8, LANES, LANES), BF16),
            pltpu.VMEM((2, 4, LANES, LANES), BF16),
            pltpu.VMEM((4, LANES, LANES), F32),
            pltpu.VMEM((8, LANES), F32),
            pltpu.VMEM((16, 8, LANES), F32),
            pltpu.VMEM((8, LANES), F32),
            pltpu.VMEM((2, 8, LANES), F32),
            pltpu.VMEM((8, LANES), F32),
            pltpu.VMEM((8, LANES), F32),
            pltpu.VMEM((16, 8, LANES), F32),
            pltpu.VMEM((ROWS, LANES), F32),
            dma((NIN + 6,)),
            dma((2, NZ // 2 + 1, NCH)), dma((2, NZ // 2 + 1, NCH)),
            dma((4,)), dma((4,)),
            dma((4, 5)), dma((4, 5)),
            dma((4, 5)), dma((3, 5)),
            dma, dma, dma((3,)), dma((3,)),
            dma((8,)), dma((2, 4)),
            dma((16,)), dma((16,)),
            dma((2,)), dma((2,)),
            dma((16,)), dma((16,)),
        ],
        compiler_params=pltpu.CompilerParams(
            collective_id=0, has_side_effects=True, vmem_limit_bytes=VMEM
        ),
        cost_estimate=pl.CostEstimate(
            flops=2 * ROWS * 2048 * KD, bytes_accessed=3 * 2**20, transcendentals=0
        ),
    )(
        train_codes, train_exps.T, train_ids.reshape(4, LANES), query_codes, query_exps.T,
        query_ids.reshape(1, BLK), precond.reshape(NBLK, LANES),
    )
    return cosines, peak.reshape(ROWS)


def solution(mesh):
    in_specs = (
        P("row", "col"),
        P("row", "col"),
        P("row"),
        P("row", "col"),
        P("row", "col"),
        P("row"),
        P("col"),
    )
    out_specs = (P("row", "col"), P("row"))
    return jax.shard_map(shards, mesh=mesh, in_specs=in_specs, out_specs=out_specs, check_vma=False)
```

time: 107 us -> 87.9 us (0.82)
  Pallas kernels: 98.7 us -> 84 us
  local copies, waits for them, and re-layouts: 7.51 us -> 2.92 us
    pallas_call x1, Pallas kernels: 98.7 us -> 84 us  [shards(): pl.pallas_call(kernel, out_shape=(jax.ShapeDtypeStruct((ROWS, LANES), F32...]
    unnamed x14 -> x2, local copies, waits for them, and re-layouts: 7.51 us -> 2.92 us
where the time goes in v2:
time: 87.9 us; the launch traced here: 87.5 us
  Pallas kernels  84 us (96%)
  local copies, waits for them, and re-layouts  2.92 us (3%)
    pallas_call x1, Pallas kernels, shards(): pl.pallas_call(kernel, out_shape=(jax.ShapeDtypeStruct((ROWS, LANES), F32...  84 us
    unnamed x2, local copies, waits for them, and re-layouts  2.92 us

profile of v2, /device:TPU:1, one launch (start us, length us, event | category | flops | bytes accessed | tf_op | source)
XLA Modules:
  0.0 87.5 jit_solution(7720889976489464335)
XLA Ops:
  0.6 84.0 %shard_map.86 = (f32[512,128]{1,0:T(8,128)}, f32[4,128]{1,0:T(4,128)}) custom-call(bf16[512,2048]{1,0:T(8,128)(2,1)} %tc_hbm.1, s32[16,512]{1,0:T(8,128)} %bitcast.7, s32[4,128]{1,0:T(4,128)} %bitcast.10, bf16[64,2048]{1,0:T(8,128)(2,1)} %qc_hbm.1, s32[16,64]{1,0:T(8,128)} %bitcast.8, s32[1,64]{1,0:T(1,128)} %bitcast.11, f32[16,128]{1,0:T(8,128)} %bitcast.9), custom_call_target="tpu_custom_call" | custom-call | flops 4294967296 | bytes 3145728 | tf_op jit(solution)/shard_map/pallas_call | solution.py:568
  84.6 1.7 %copy.11 = f32[512,128]{1,0:T(8,128)} copy(f32[512,128]{1,0:T(8,128)} %get-tuple-element.8) | data formatting | bytes 524288
  86.3 1.2 %copy.12 = f32[512]{0:T(512)} copy(f32[512]{0:T(512)} %bitcast.6) | data formatting | bytes 4096

commit v3 on v2

--- a/solution.py
+++ b/solution.py
@@ -20,7 +20,7 @@
 ROWS = 512
 LANES = 128
 NBLK = KD // LANES
-NCH = 4
+NCH = 2
 CH = BLK // NCH
 XCH = 16
 NX = ROWS // XCH
@@ -51,9 +51,9 @@
 
 def kernel(
     tc_hbm, te_hbm, tid_hbm, qc_hbm, qe_hbm, qid_hbm, pre_hbm,
-    cos_hbm, peak_ref,
+    cos_ref, peaks,
     tcode, texp, tfac, tid_ref, qcode, qexp, qid_ref, pre_ref, a_all, b_all, tsq, prod, r1, s2, r2, acc, sx, rx, keep,
-    mine, parts, meta, metas, tinv, ppart, peaks, cosv,
+    mine, parts, meta, metas, tinv, ppart,
     in_sem, z_send, z_recv, x_send, x_recv, s1_send, s1_recv, s2_send, s2_recv, n1_send, n1_recv, n2_send, n2_recv,
     s3_send, s3_recv, a_send, a_recv, m_send, m_recv, p_send, p_recv,
 ):
@@ -68,28 +68,31 @@
     twin = (r, c + 1 - 2 * core)
     home = xhi == xlo
 
-    barrier = pltpu.get_barrier_semaphore()
-    for peer in (up, down, xpair, diag):
-        pl.semaphore_signal(barrier, inc=1, device_id=peer, device_id_type=MESH)
-
-    def greet(k, _):
-        pl.semaphore_signal(barrier, inc=1, device_id=(r, lax.rem(c + k, 16)), device_id_type=MESH)
-        return 0
-
-    lax.fori_loop(1, 16, greet, 0)
-    is_self = [jnp.logical_and(2 * c + i == r, lax.div(r, 2) == c) for i in range(2)]
-    for i in range(2):
-        @pl.when(jnp.logical_not(is_self[i]))
-        def _():
-            pl.semaphore_signal(barrier, inc=1, device_id=(2 * c + i, lax.div(r, 2)), device_id_type=MESH)
-
     first_in = [
         pltpu.make_async_copy(src, dst, in_sem.at[NIN + i])
         for i, (src, dst) in enumerate(
             [(qc_hbm, qcode), (qe_hbm, qexp), (pre_hbm, pre_ref), (te_hbm, texp), (tid_hbm, tid_ref), (qid_hbm, qid_ref)]
         )
     ]
-    for copy in first_in:
+    for copy in first_in[:3]:
+        copy.start()
+
+    barrier = pltpu.get_barrier_semaphore()
+    for peer in (up, down, xpair, diag):
+        pl.semaphore_signal(barrier, inc=1, device_id=peer, device_id_type=MESH)
+
+    def greet(k, _):
+        pl.semaphore_signal(barrier, inc=1, device_id=(r, lax.rem(c + k, 16)), device_id_type=MESH)
+        return 0
+
+    lax.fori_loop(1, 16, greet, 0)
+    is_self = [jnp.logical_and(2 * c + i == r, lax.div(r, 2) == c) for i in range(2)]
+    for i in range(2):
+        @pl.when(jnp.logical_not(is_self[i]))
+        def _():
+            pl.semaphore_signal(barrier, inc=1, device_id=(2 * c + i, lax.div(r, 2)), device_id_type=MESH)
+
+    for copy in first_in[3:]:
         copy.start()
 
     def t_in(i):
@@ -120,12 +123,17 @@
     def z_copy(way, step, k):
         block, to = (wrap(z - step + 1), up) if way == 0 else (wrap(z + step - 1), down)
         rows = b_all.at[z_rows(block, k)]
-        return rcopy(rows, rows, z_send.at[way, step, k], z_recv.at[way, step, k], to)
+        return rcopy(rows, rows, z_send.at[way, step], z_recv.at[way, step, k], to)
 
     def z_arrival(way, step, k):
         block = wrap(z - step) if way == 0 else wrap(z + step)
         rows = b_all.at[z_rows(block, k)]
-        return rcopy(rows, rows, z_send.at[way, step, k], z_recv.at[way, step, k], up)
+        return rcopy(rows, rows, z_send.at[way, step], z_recv.at[way, step, k], up)
+
+    def z_left(step, rows):
+        for way in range(2):
+            whole_block = b_all.at[pl.ds(0, rows)]
+            rcopy(whole_block, whole_block, z_send.at[way, step], z_recv.at[way, step, 0], up).wait_send()
 
     def chunk_of(way, k):
         return k if way == 0 else (k + NCH // 2) % NCH
@@ -177,11 +185,11 @@
     mine[4:5, :] = jnp.sum(wide.T, axis=0, keepdims=True)
 
     def to_col(src, dst, send, recv, k):
-        return rcopy(src, dst.at[c], send.at[k], recv.at[c], (r, lax.rem(c + k, 16)))
-
-    def from_col(src, dst, send, recv, k):
-        who = lax.rem(c + k, 16)
-        return rcopy(src, dst.at[who], send.at[k], recv.at[who], (r, who))
+        return rcopy(src, dst.at[c], send, recv, (r, lax.rem(c + k, 16)))
+
+    def all_of_col(dst, send, recv):
+        fifteen = dst.at[pl.ds(0, 15)]
+        return rcopy(fifteen, fifteen, send, recv, twin)
 
     def send_parts(k, _):
         to_col(mine, parts, a_send, a_recv, k).start()
@@ -194,11 +202,7 @@
         return rcopy(meta, metas.at[lax.rem(r, 2)], m_send.at[i], m_recv.at[lax.rem(r, 2)], (2 * c + i, lax.div(r, 2)))
 
     def norms():
-        def got(k, _):
-            from_col(mine, parts, a_send, a_recv, k).wait_recv()
-            return 0
-
-        lax.fori_loop(1, 16, got, 0)
+        all_of_col(parts, a_send, a_recv).wait()
         total = parts[0]
         for k in range(1, 16):
             total += parts[k]
@@ -242,12 +246,12 @@
         w, q = part
         k = lax.rem(y - yd + 4, 4) - 1
         return rcopy(
-            s2.at[yd, w, q], r2.at[k, w, q], s2_send.at[yd, i], s2_recv.at[k, i], (r, xhi * 8 + yd * 2 + core)
+            s2.at[yd, w, q], r2.at[k, w, q], s2_send.at[yd, i], s2_recv.at[i], (r, xhi * 8 + yd * 2 + core)
         )
 
-    def s2_arrival(k, part, i):
+    def s2_arrival(part, i):
         w, q = part
-        return rcopy(r2.at[k, w, q], r2.at[k, w, q], s2_send.at[0, i], s2_recv.at[k, i], twin)
+        return rcopy(r2.at[:, w, q], r2.at[:, w, q], s2_send.at[0, i], s2_recv.at[i], twin)
 
     def dot(step, part):
         w, q = part
@@ -311,8 +315,11 @@
     def newest_on(n):
         yd = lax.rem(y + n, 4)
         return rcopy(
-            s2.at[yd, 7], r2.at[3 - n, 7], n2_send.at[n - 1], n2_recv.at[3 - n], (r, xhi * 8 + yd * 2 + core)
+            s2.at[yd, 7], r2.at[3 - n, 7], n2_send, n2_recv, (r, xhi * 8 + yd * 2 + core)
         )
+
+    def newest_all():
+        return rcopy(r2.at[:, 7], r2.at[:, 7], n2_send, n2_recv, twin)
 
     def work_newest():
         x_group(3).wait_recv()
@@ -331,7 +338,10 @@
             newest_on(n).start()
         acc[7] = prod[y, core, 7] + r1[y, 7]
 
-    def arrive(step, k):
+    def arrive(step, slot):
+        if slot % (4 // NCH):
+            return
+        k = slot // (4 // NCH)
         for way in range(2):
             chunk = chunk_of(way, k)
 
@@ -344,13 +354,16 @@
                 z_copy(way, step + 1, chunk).start()
 
     def follow(step, k):
-        i = (step - 1) * NCH + k + XLEAD
+        i = (step - 1) * 4 + k + XLEAD
 
         @pl.when(i < NX)
         def _():
             x_copy(i).start()
 
     own = whole(0, 4)
+    most = whole(0, 7)
+    first = half(0, 7, soon)
+    ends = (half(0, 4, late), half(4, 7, late))
 
     def body(step, _):
         arrive(step, 0)
@@ -370,6 +383,7 @@
         @pl.when(step > 1)
         def _():
             old(step - 1, relay)
+            z_left(step - 1, BLK)
 
         new(step - 1, relay)
 
@@ -379,41 +393,58 @@
 
         arrive(step, 3)
         follow(step, 3)
-        work(step, own, 0)
+
+        @pl.when(step < last - 1)
+        def _():
+            work(step, own, 0)
+
         return 0
 
     lax.fori_loop(1, last, body, 0)
+
+    yd7, cd7 = pair_at(last - 1)
+    yd8, cd8 = pair_at(last)
+    at7 = pl.ds(pl.multiple_of((2 * yd7 + cd7) * LANES, LANES), LANES)
+    at8 = pl.ds(pl.multiple_of((2 * yd8 + cd8) * LANES + soon, BLK), BLK)
+    value = lax.dot_general(
+        jnp.concatenate([b_all[at7, :], b_all[at8, :]], axis=0), a_all[pl.ds(0, 7 * LANES), :],
+        (((1,), (1,)), ((), ())), preferred_element_type=F32,
+    )
+    for n in range(7):
+        prod[yd7, cd7, n] = value[:LANES, n * LANES : (n + 1) * LANES]
+        prod[yd8, cd8, n, first[1], :] = value[LANES:, n * LANES : (n + 1) * LANES]
+    for step, part in ((last - 1, most), (last, first)):
+        @pl.when(core != pair_at(step)[1])
+        def _():
+            s1_copy(pair_at(step)[0], part, 0).start()
+
     arrive(last, 0)
-    old(last - 1, work)
-    relay(last - 1, own, 0)
-    work(last, half(0, 4, soon), 0)
+    relay(last - 1, most, 0)
+    relay(last, first, 0)
     arrive(last, 1)
-    work(last, half(0, 4, late), 1)
-    old(last - 1, relay)
-    relay(last, half(0, 4, soon), 0)
-    work(last, half(4, 7, soon), 2)
-    relay(last, half(0, 4, late), 1)
-    work(last, half(4, 7, late), 3)
+    work(last, ends[0], 1)
+    work(last, ends[1], 2)
+    relay(last, ends[0], 1)
+    relay(last, ends[1], 2)
     work_newest()
-    relay(last, half(4, 7, soon), 2)
-    relay(last, half(4, 7, late), 3)
     relay_newest()
 
-    lyd, lcd = pair_at(last)
-    is_last = jnp.logical_and(y == lyd, core == lcd)
-
-    def y_arrived(parts_last, parts_else):
-        @pl.when(is_last)
-        def _():
-            for k in range(3):
-                for part, i in parts_last:
-                    s2_arrival(k, part, i).wait_recv()
-
-        @pl.when(jnp.logical_not(is_last))
-        def _():
-            for k in range(3):
-                for part, i in parts_else:
-                    s2_arrival(k, part, i).wait_recv()
+    j_last, j_before = pair_of(z, last), pair_of(z, last - 1)
+    of_own = ([(first, 0), (ends[0], 1)], [(most, 0)], [(own, 0)])
+    of_old = ([(ends[1], 2)], [], [(group(4 + g), 2 + g) for g in range(3)])
+
+    def by_pair(j, cases, do):
+        is_one, is_two = j == j_last, j == j_before
+        tests = (is_one, is_two, jnp.logical_not(jnp.logical_or(is_one, is_two)))
+        for test, some in zip(tests, cases):
+            if some:
+                @pl.when(test)
+                def _():
+                    for part, i in some:
+                        do(part, i)
+
+    def y_arrived(cases):
+        by_pair(2 * y + core, cases, lambda part, i: s2_arrival(part, i).wait_recv())
 
     def summed(w):
         return acc[w] + r2[0, w].astype(F32) + r2[1, w].astype(F32) + r2[2, w].astype(F32)
@@ -427,9 +458,7 @@
     def s3_diag(u):
         return rcopy(sx.at[4 + u], rx.at[1, u], s3_send.at[4 + u], s3_recv.at[1, u], diag)
 
-    own_parts = ([(half(0, 4, soon), 0), (half(0, 4, late), 1)], [(own, 0)])
-    old_parts = ([(half(4, 7, soon), 2), (half(4, 7, late), 3)], [(group(4 + g), 2 + g) for g in range(3)])
-    y_arrived(*own_parts)
+    y_arrived(of_own)
     for u in range(4):
         total = summed(u)
 
@@ -444,10 +473,9 @@
 
     for u in range(4):
         if u == 0:
-            y_arrived(*old_parts)
+            y_arrived(of_old)
         if u == 3:
-            for n in (1, 2, 3):
-                newest_on(n).wait_recv()
+            newest_all().wait_recv()
         sx[4 + u] = summed(4 + u).astype(BF16)
 
         @pl.when(home)
@@ -457,6 +485,30 @@
         @pl.when(jnp.logical_not(home))
         def _():
             s3_diag(u).start()
+
+    def left(yd, _):
+        def out(copy, j):
+            by_pair(j, [a + b for a, b in zip(of_own, of_old)], lambda part, i: copy(yd, part, i).wait_send())
+
+        out(s1_copy, 2 * yd + 1 - core)
+
+        @pl.when(yd != y)
+        def _():
+            out(s2_copy, 2 * yd + core)
+
+        return 0
+
+    lax.fori_loop(0, 4, left, 0)
+    z_left(last - 1, BLK)
+    z_left(last, BLK // 2)
+    for g in range(4):
+        x_group(g).wait_send()
+    newest_copy().wait_send()
+    newest_all().wait_send()
+    for i in range(2):
+        @pl.when(jnp.logical_not(is_self[i]))
+        def _():
+            meta_copy(i).wait_send()
 
     for i in range(2):
         @pl.when(jnp.logical_not(is_self[i]))
@@ -469,10 +521,6 @@
     q_ids = jnp.broadcast_to(both[1:2, :], (LANES, LANES)).T
     t_ids = tid_ref[...].astype(F32)
 
-    def out_copy(u):
-        rows = pl.ds(u * LANES, LANES)
-        return pltpu.make_async_copy(cosv.at[rows], cos_hbm.at[rows], in_sem.at[u])
-
     ppart[...] = jnp.zeros_like(ppart)
     for u in range(4):
         s3_pair(u).wait_recv()
@@ -486,7 +534,7 @@
         value = raw * q_inv * tinv[u : u + 1, :]
         value = jnp.where(q_ids == t_ids[u : u + 1, :], 0.0, value)
         ppart[u : u + 1, :] = jnp.max(value, axis=0, keepdims=True)
-        cosv[pl.ds(u * LANES, LANES), :] = value.T
+        cos_ref[u] = value
 
     def send_peaks(k, _):
         to_col(ppart, peaks, p_send, p_recv, k).start()
@@ -495,81 +543,33 @@
     lax.fori_loop(1, 16, send_peaks, 0)
     peaks[c] = ppart[...]
     for u in range(4):
-        out_copy(u).start()
-
-    def sent(step, _):
-        for k in range(NCH):
-            for way in range(2):
-                z_copy(way, step, k).wait_send()
-        return 0
-
-    lax.fori_loop(1, NZ // 2, sent, 0)
-    for k in range(NCH // 2):
-        for way in range(2):
-            z_copy(way, NZ // 2, chunk_of(way, k)).wait_send()
-
-    def x_sent(i, _):
-        x_group(i).wait_send()
-        return 0
-
-    lax.fori_loop(0, 4, x_sent, 0)
-
-    def s_sent(yd, _):
-        def out(copy, j):
-            for of_last, some in ((True, own_parts[0] + old_parts[0]), (False, own_parts[1] + old_parts[1])):
-                @pl.when((j == pair_of(z, last)) == of_last)
-                def _():
-                    for part, i in some:
-                        copy(yd, part, i).wait_send()
-
-        out(s1_copy, 2 * yd + 1 - core)
-
-        @pl.when(yd != y)
-        def _():
-            out(s2_copy, 2 * yd + core)
-
-        return 0
-
-    lax.fori_loop(0, 4, s_sent, 0)
-    newest_copy().wait_send()
-    for n in (1, 2, 3):
-        newest_on(n).wait_send()
+        @pl.when(jnp.logical_not(home))
+        def _():
+            s3_own(u).wait_send()
+
+        s3_pair(u).wait_send()
+
+    all_of_col(peaks, p_send, p_recv).wait()
+
+
+def lay_out(tiles, peaks, cos_ref, peak_ref):
     for u in range(4):
-        @pl.when(jnp.logical_not(home))
-        def _():
-            s3_own(u).wait_send()
-
-        s3_pair(u).wait_send()
-
-    for i in range(2):
-        @pl.when(jnp.logical_not(is_self[i]))
-        def _():
-            meta_copy(i).wait_send()
-
-    def col_done(k, _):
-        to_col(mine, parts, a_send, a_recv, k).wait_send()
-        to_col(ppart, peaks, p_send, p_recv, k).wait_send()
-        from_col(ppart, peaks, p_send, p_recv, k).wait_recv()
-        return 0
-
-    lax.fori_loop(1, 16, col_done, 0)
+        cos_ref[pl.ds(u * LANES, LANES), :] = tiles[u].T
     best = peaks[0]
     for k in range(1, 16):
         best = jnp.maximum(best, peaks[k])
     peak_ref[...] = best[0:4, :]
-    for u in range(4):
-        out_copy(u).wait()
 
 
 def shards(train_codes, train_exps, train_ids, query_codes, query_exps, query_ids, precond):
     dma = pltpu.SemaphoreType.DMA
     vmem = pl.BlockSpec(memory_space=pltpu.VMEM)
     hbm = pl.BlockSpec(memory_space=pl.ANY)
-    cosines, peak = pl.pallas_call(
+    tiles, peaks = pl.pallas_call(
         kernel,
-        out_shape=(jax.ShapeDtypeStruct((ROWS, LANES), F32), jax.ShapeDtypeStruct((4, LANES), F32)),
+        out_shape=(pltpu.VMEM((4, LANES, LANES), F32), pltpu.VMEM((16, 8, LANES), F32)),
         in_specs=[hbm] * 7,
-        out_specs=(hbm, vmem),
+        out_specs=(vmem, vmem),
         scratch_shapes=[
             pltpu.VMEM((ROWS, KD), BF16),
             pltpu.VMEM((NBLK, ROWS), jnp.int32),
@@ -596,18 +596,16 @@
             pltpu.VMEM((2, 8, LANES), F32),
             pltpu.VMEM((8, LANES), F32),
             pltpu.VMEM((8, LANES), F32),
-            pltpu.VMEM((16, 8, LANES), F32),
-            pltpu.VMEM((ROWS, LANES), F32),
             dma((NIN + 6,)),
-            dma((2, NZ // 2 + 1, NCH)), dma((2, NZ // 2 + 1, NCH)),
+            dma((2, NZ // 2 + 1)), dma((2, NZ // 2 + 1, NCH)),
             dma((4,)), dma((4,)),
             dma((4, 5)), dma((4, 5)),
-            dma((4, 5)), dma((3, 5)),
-            dma, dma, dma((3,)), dma((3,)),
+            dma((4, 5)), dma((5,)),
+            dma, dma, dma, dma,
             dma((8,)), dma((2, 4)),
-            dma((16,)), dma((16,)),
+            dma, dma,
             dma((2,)), dma((2,)),
-            dma((16,)), dma((16,)),
+            dma, dma,
         ],
         compiler_params=pltpu.CompilerParams(
             collective_id=0, has_side_effects=True, vmem_limit_bytes=VMEM
@@ -619,6 +617,12 @@
         train_codes, train_exps.T, train_ids.reshape(4, LANES), query_codes, query_exps.T,
         query_ids.reshape(1, BLK), precond.reshape(NBLK, LANES),
     )
+    cosines, peak = pl.pallas_call(
+        lay_out,
+        out_shape=(jax.ShapeDtypeStruct((ROWS, LANES), F32), jax.ShapeDtypeStruct((4, LANES), F32)),
+        in_specs=[vmem, vmem],
+        out_specs=(vmem, vmem),
+    )(tiles, peaks)
     return cosines, peak.reshape(ROWS)
 
 

time: 87.9 us -> 86.2 us (0.981)
  local copies, waits for them, and re-layouts: 2.92 us -> 1.31 us
  Pallas kernels: 84 us -> 83.1 us
    unnamed x2 -> x4, local copies, waits for them, and re-layouts: 2.92 us -> 1.31 us
    pallas_call x1 -> x2, Pallas kernels: 84 us -> 83.1 us  [the longest x1 81.3 us: shards(): pl.pallas_call(kernel, out_shape=(pltpu.VMEM((4, LANES, LANES), F32), plt...]
where the time goes in v3:
time: 86.2 us; the launch traced here: 85 us
  Pallas kernels  83.1 us (96%)
  local copies, waits for them, and re-layouts  1.31 us (2%)
    pallas_call x1, Pallas kernels, shards(): pl.pallas_call(kernel, out_shape=(pltpu.VMEM((4, LANES, LANES), F32), plt...  81.3 us
    pallas_call x1, Pallas kernels, shards(): pl.pallas_call(lay_out, out_shape=(jax.ShapeDtypeStruct((ROWS, LANES), F3...  1.79 us

profile of v3, /device:TPU:1, one launch (start us, length us, event | category | flops | bytes accessed | tf_op | source)
XLA Modules:
  0.0 85.0 jit_solution(879751585195246832)
XLA Ops:
  0.6 81.3 %shard_map.86 = (f32[4,128,128]{2,1,0:T(8,128)S(1)}, f32[16,8,128]{2,1,0:T(8,128)S(1)}) custom-call(bf16[512,2048]{1,0:T(8,128)(2,1)} %tc_hbm.1, s32[16,512]{1,0:T(8,128)} %bitcast.6, s32[4,128]{1,0:T(4,128)} %bitcast.9, bf16[64,2048]{1,0:T(8,128)(2,1)} %qc_hbm.1, s32[16,64]{1,0:T(8,128)} %bitcast.7, s32[1,64]{1,0:T(1,128)} %bitcast.11, f32[16,128]{1,0:T(8,128)} %bitcast.8), custom_call_target="tpu_custom_call" | custom-call | flops 4294967296 | bytes 3145728 | tf_op jit(solution)/shard_map/pallas_call | solution.py:568
  81.9 0.0 copy-start
  81.9 0.7 copy-done
  82.6 0.0 copy-start.1
  82.6 0.6 copy-done.1
  83.3 1.8 %shard_map.87 = (f32[512,128]{1,0:T(8,128)}, f32[4,128]{1,0:T(4,128)}) custom-call(f32[4,128,128]{2,1,0:T(8,128)} %copy-done, f32[16,8,128]{2,1,0:T(8,128)} %copy-done.1), custom_call_target="tpu_custom_call" | custom-call | tf_op jit(solution)/shard_map/pallas_call | solution.py:620
Async XLA Ops:
  81.9 0.7 copy-start
  82.6 0.6 copy-start.1

commit v4 on v3

--- a/solution.py
+++ b/solution.py
@@ -20,7 +20,7 @@
 ROWS = 512
 LANES = 128
 NBLK = KD // LANES
-NCH = 2
+NCH = 4
 CH = BLK // NCH
 XCH = 16
 NX = ROWS // XCH
@@ -52,10 +52,10 @@
 def kernel(
     tc_hbm, te_hbm, tid_hbm, qc_hbm, qe_hbm, qid_hbm, pre_hbm,
     cos_ref, peaks,
-    tcode, texp, tfac, tid_ref, qcode, qexp, qid_ref, pre_ref, a_all, b_all, tsq, prod, r1, s2, r2, acc, sx, rx, keep,
-    mine, parts, meta, metas, tinv, ppart,
-    in_sem, z_send, z_recv, x_send, x_recv, s1_send, s1_recv, s2_send, s2_recv, n1_send, n1_recv, n2_send, n2_recv,
-    s3_send, s3_recv, a_send, a_recv, m_send, m_recv, p_send, p_recv,
+    tcode, texp, tfac, tid_ref, qcode, qexp, qid_ref, pre_ref, a_all, b_all, tsq, prod, r1, s2, r2, rf, acc, sx, rx, keep,
+    mine, parts, tots, metas, qparts, mtot, mpair, tinv, ppart,
+    in_sem, z_send, z_recv, x_send, x_recv, s1_send, s1_recv, s2_send, s2_recv, c_send, c_recv, f_recv, n1_send, n1_recv, n2_send, n2_recv,
+    s3_send, s3_recv, t_send, t_recv, m_send, m_recv, mp_send, mp_recv, q_send, q_recv, p_send, p_recv,
 ):
     r, c = lax.axis_index("row"), lax.axis_index("col")
     xlo, z = lax.div(r, NZ), lax.rem(r, NZ)
@@ -68,6 +68,10 @@
     twin = (r, c + 1 - 2 * core)
     home = xhi == xlo
 
+    def y_dev(to):
+        return (r, xhi * 8 + lax.rem(to, 4) * 2 + core)
+
+
     first_in = [
         pltpu.make_async_copy(src, dst, in_sem.at[NIN + i])
         for i, (src, dst) in enumerate(
@@ -78,19 +82,8 @@
         copy.start()
 
     barrier = pltpu.get_barrier_semaphore()
-    for peer in (up, down, xpair, diag):
+    for peer in (up, down, xpair, diag, xhop, twin, y_dev(y + 1), y_dev(y + 2), y_dev(y + 3)):
         pl.semaphore_signal(barrier, inc=1, device_id=peer, device_id_type=MESH)
-
-    def greet(k, _):
-        pl.semaphore_signal(barrier, inc=1, device_id=(r, lax.rem(c + k, 16)), device_id_type=MESH)
-        return 0
-
-    lax.fori_loop(1, 16, greet, 0)
-    is_self = [jnp.logical_and(2 * c + i == r, lax.div(r, 2) == c) for i in range(2)]
-    for i in range(2):
-        @pl.when(jnp.logical_not(is_self[i]))
-        def _():
-            pl.semaphore_signal(barrier, inc=1, device_id=(2 * c + i, lax.div(r, 2)), device_id_type=MESH)
 
     for copy in first_in[3:]:
         copy.start()
@@ -113,9 +106,12 @@
         b_all[pl.ds(mine_at, BLK), cols] = value
         qsq += jnp.square(value.astype(F32))
 
-    pl.semaphore_wait(
-        barrier, 4 + 15 + 2 - is_self[0].astype(jnp.int32) - is_self[1].astype(jnp.int32)
-    )
+    first_in[5].wait()
+    wide = jnp.concatenate([qsq, jnp.zeros_like(qsq)], axis=0)
+    metas[z] = jnp.zeros((8, LANES), F32)
+    metas[z, 0:1, :] = jnp.sum(wide.T, axis=0, keepdims=True)
+    metas[z, 1:2, 0:BLK] = qid_ref[...].astype(F32)
+    pl.semaphore_wait(barrier, 9)
 
     def z_rows(block, k):
         return pl.ds(pl.multiple_of(block * BLK + k * CH, CH), CH)
@@ -138,9 +134,27 @@
     def chunk_of(way, k):
         return k if way == 0 else (k + NCH // 2) % NCH
 
+    def m_copy(way, hop):
+        block, to = (wrap(z - hop + 1), up) if way == 0 else (wrap(z + hop - 1), down)
+        return rcopy(metas.at[block], metas.at[block], m_send.at[way], m_recv.at[way, hop], to)
+
+    def m_pass(hop):
+        for way in range(2):
+            block = wrap(z - hop) if way == 0 else wrap(z + hop)
+
+            @pl.when(hop + way <= NZ // 2)
+            def _():
+                rcopy(metas.at[block], metas.at[block], m_send.at[way], m_recv.at[way, hop], up).wait_recv()
+
+            @pl.when(hop + way < NZ // 2)
+            def _():
+                m_copy(way, hop + 1).start()
+
     for k in range(NCH):
         for way in range(2):
             z_copy(way, 1, chunk_of(way, k)).start()
+            if k == 1:
+                m_copy(way, 1).start()
 
     def x_copy(i):
         rows = pl.ds(pl.multiple_of(i * XCH, XCH), XCH)
@@ -153,7 +167,7 @@
         there = pl.ds(pl.multiple_of(ROWS + g * LANES, LANES), LANES)
         return rcopy(a_all.at[rows], a_all.at[there], x_send.at[g], x_recv.at[g], xpair)
 
-    for copy in first_in[3:]:
+    for copy in first_in[3:5]:
         copy.wait()
     tfac[...] = power(texp[...]).T
 
@@ -181,8 +195,6 @@
     mine[...] = jnp.zeros_like(mine)
     for g in range(4):
         mine[g : g + 1, :] = jnp.sum(tsq[pl.ds(g * LANES, LANES), :].T, axis=0, keepdims=True)
-    wide = jnp.concatenate([qsq, jnp.zeros_like(qsq)], axis=0)
-    mine[4:5, :] = jnp.sum(wide.T, axis=0, keepdims=True)
 
     def to_col(src, dst, send, recv, k):
         return rcopy(src, dst.at[c], send, recv, (r, lax.rem(c + k, 16)))
@@ -191,33 +203,62 @@
         fifteen = dst.at[pl.ds(0, 15)]
         return rcopy(fifteen, fifteen, send, recv, twin)
 
-    def send_parts(k, _):
-        to_col(mine, parts, a_send, a_recv, k).start()
-        return 0
-
-    lax.fori_loop(1, 16, send_parts, 0)
-    parts[c] = mine[...]
-
-    def meta_copy(i):
-        return rcopy(meta, metas.at[lax.rem(r, 2)], m_send.at[i], m_recv.at[lax.rem(r, 2)], (2 * c + i, lax.div(r, 2)))
-
-    def norms():
-        all_of_col(parts, a_send, a_recv).wait()
-        total = parts[0]
-        for k in range(1, 16):
-            total += parts[k]
-        tinv[...] = math.sqrt(P_SIZE) / jnp.sqrt(total + EPS)
-        meta[...] = jnp.zeros_like(meta)
-        meta[0:1, :] = total[4:5, :]
-        meta[1:2, 0:BLK] = qid_ref[...].astype(F32)
-        for i in range(2):
-            @pl.when(is_self[i])
-            def _():
-                metas[i] = meta[...]
-
-            @pl.when(jnp.logical_not(is_self[i]))
-            def _():
-                meta_copy(i).start()
+    def t_copy(k):
+        src, to = (mine, twin) if k == 0 else (tots.at[1], xhop) if k == 4 else (tots.at[0], y_dev(y + k))
+        return rcopy(src, parts.at[k], t_send.at[k], t_recv.at[k], to)
+
+    t_copy(0).start()
+
+    def q_copy(n):
+        return rcopy(metas.at[pl.ds(2 * n, 2)], qparts.at[c], q_send, q_recv, (r, 8 * xlo + n))
+
+    def q_sent(count):
+        some = qparts.at[pl.ds(0, count)]
+        return rcopy(some, some, q_send, q_recv, twin)
+
+    def m_pair():
+        return rcopy(mtot, mpair, mp_send, mp_recv, xpair)
+
+    def send_shares():
+        def one(n, _):
+            @pl.when(8 * xlo + n != c)
+            def _():
+                q_copy(n).start()
+
+            return 0
+
+        lax.fori_loop(0, 8, one, 0)
+
+        @pl.when(home)
+        def _():
+            qparts[c] = metas[pl.ds(4 * y + 2 * core, 2)]
+
+    def sum_shares():
+        @pl.when(home)
+        def _():
+            q_sent(15).wait_recv()
+            total = qparts[0]
+            for k in range(1, 16):
+                total += qparts[k]
+            row = lax.broadcasted_iota(jnp.int32, total.shape, 1)
+            mtot[...] = jnp.where(row == 0, total, metas[pl.ds(4 * y + 2 * core, 2)])
+            m_pair().start()
+            mpair[...] = mtot[...]
+
+    def norms(phase):
+        if phase == 1:
+            t_copy(0).wait_recv()
+            tots[0] = mine[...] + parts[0]
+            for k in (1, 2, 3):
+                t_copy(k).start()
+        elif phase == 2:
+            for k in (1, 2, 3):
+                t_copy(k).wait_recv()
+            tots[1] = tots[0] + parts[1] + parts[2] + parts[3]
+            t_copy(4).start()
+        else:
+            t_copy(4).wait_recv()
+            tinv[...] = math.sqrt(P_SIZE) / jnp.sqrt(tots[1] + parts[4] + EPS)
 
     last = NZ // 2
     late = lax.rem(z, 2) * BLK
@@ -252,6 +293,59 @@
     def s2_arrival(part, i):
         w, q = part
         return rcopy(r2.at[:, w, q], r2.at[:, w, q], s2_send.at[0, i], s2_recv.at[i], twin)
+
+    def cut(part, k):
+        w, q = part
+        n = q.size // 2
+        at_once = q.start + jnp.where(k == 1, 0, n)
+        later = q.start + jnp.where(k == 1, n, 0)
+        return (w, pl.ds(pl.multiple_of(at_once, n), n)), (w, pl.ds(pl.multiple_of(later, n), n))
+
+    def far_copy(yd, part, i, k):
+        (w, q), to = cut(part, k)[1], yd + k
+        return rcopy(s2.at[yd, w, q], rf.at[w, q], c_send.at[i], f_recv.at[i], y_dev(to))
+
+    def near_copy(yd, part, i, k):
+        w, q = part
+        return rcopy(s2.at[yd, w, q], r2.at[lax.div(k, 2), w, q], c_send.at[i], c_recv.at[i], y_dev(yd))
+
+    def chain_at(step):
+        yd, cd = pair_at(step)
+        return yd, cd, lax.rem(y - yd + 4, 4)
+
+    def chain(step, part, i):
+        w, q = part
+        yd, cd, k = chain_at(step)
+
+        @pl.when(core == cd)
+        def _():
+            s1_copy(yd, part, i).wait_recv()
+
+            @pl.when(k == 0)
+            def _():
+                acc[w, q, :] = prod[yd, cd, w, q, :] + r1[yd, w, q, :]
+
+            @pl.when(k == 2)
+            def _():
+                s2[yd, w, q, :] = (prod[yd, cd, w, q, :] + r1[yd, w, q, :]).astype(BF16)
+                far_copy(yd, part, i, 1).start()
+                far_copy(yd, part, i, 3).start()
+
+            @pl.when(lax.rem(k, 2) == 1)
+            def _():
+                h = cut(part, k)[0]
+                s2[yd, w, h[1], :] = (prod[yd, cd, w, h[1], :] + r1[yd, w, h[1], :]).astype(BF16)
+                near_copy(yd, h, i, k).start()
+
+    def chain_end(step, part, i):
+        yd, cd, k = chain_at(step)
+
+        @pl.when(jnp.logical_and(core == cd, lax.rem(k, 2) == 1))
+        def _():
+            w, q = cut(part, k)[1]
+            rcopy(rf.at[w, q], rf.at[w, q], c_send.at[i], f_recv.at[i], twin).wait_recv()
+            s2[yd, w, q, :] = (prod[yd, cd, w, q, :] + r1[yd, w, q, :] + rf[w, q, :].astype(F32)).astype(BF16)
+            near_copy(yd, (w, q), i, k).start()
 
     def dot(step, part):
         w, q = part
@@ -338,10 +432,7 @@
             newest_on(n).start()
         acc[7] = prod[y, core, 7] + r1[y, 7]
 
-    def arrive(step, slot):
-        if slot % (4 // NCH):
-            return
-        k = slot // (4 // NCH)
+    def arrive(step, k):
         for way in range(2):
             chunk = chunk_of(way, k)
 
@@ -353,8 +444,11 @@
             def _():
                 z_copy(way, step + 1, chunk).start()
 
+        if k == 1:
+            m_pass(step)
+
     def follow(step, k):
-        i = (step - 1) * 4 + k + XLEAD
+        i = (step - 1) * NCH + k + XLEAD
 
         @pl.when(i < NX)
         def _():
@@ -387,9 +481,10 @@
 
         new(step - 1, relay)
 
-        @pl.when(step == 2)
-        def _():
-            norms()
+        for phase in (1, 2, 3):
+            @pl.when(step == phase)
+            def _():
+                norms(phase)
 
         arrive(step, 3)
         follow(step, 3)
@@ -418,11 +513,22 @@
         def _():
             s1_copy(pair_at(step)[0], part, 0).start()
 
+    @pl.when(2 * y + core == pair_of(z, last - 1))
+    def _():
+        r2[2, most[0], most[1], :] = jnp.zeros((7, LANES, LANES), BF16)
+
+    @pl.when(2 * y + core == pair_of(z, last))
+    def _():
+        r2[2, first[0], first[1], :] = jnp.zeros((7, BLK, LANES), BF16)
+
     arrive(last, 0)
-    relay(last - 1, most, 0)
-    relay(last, first, 0)
+    chain(last - 1, most, 0)
+    chain(last, first, 0)
     arrive(last, 1)
     work(last, ends[0], 1)
+    send_shares()
+    chain_end(last - 1, most, 0)
+    chain_end(last, first, 0)
     work(last, ends[1], 2)
     relay(last, ends[0], 1)
     relay(last, ends[1], 2)
@@ -430,7 +536,8 @@
     relay_newest()
 
     j_last, j_before = pair_of(z, last), pair_of(z, last - 1)
-    of_own = ([(first, 0), (ends[0], 1)], [(most, 0)], [(own, 0)])
+    of_chain = ([(first, 0)], [(most, 0)], [])
+    of_own = ([(ends[0], 1)], [], [(own, 0)])
     of_old = ([(ends[1], 2)], [], [(group(4 + g), 2 + g) for g in range(3)])
 
     def by_pair(j, cases, do):
@@ -443,6 +550,11 @@
                     for part, i in some:
                         do(part, i)
 
+    def c_arrival(part, i):
+        w, q = part
+        two = r2.at[pl.ds(0, 2), w, q]
+        return rcopy(two, two, c_send.at[i], c_recv.at[i], twin)
+
     def y_arrived(cases):
         by_pair(2 * y + core, cases, lambda part, i: s2_arrival(part, i).wait_recv())
 
@@ -458,6 +570,7 @@
     def s3_diag(u):
         return rcopy(sx.at[4 + u], rx.at[1, u], s3_send.at[4 + u], s3_recv.at[1, u], diag)
 
+    by_pair(2 * y + core, of_chain, lambda part, i: c_arrival(part, i).wait_recv())
     y_arrived(of_own)
     for u in range(4):
         total = summed(u)
@@ -486,15 +599,30 @@
         def _():
             s3_diag(u).start()
 
+    sum_shares()
+
     def left(yd, _):
         def out(copy, j):
-            by_pair(j, [a + b for a, b in zip(of_own, of_old)], lambda part, i: copy(yd, part, i).wait_send())
+            by_pair(
+                j, [a + b + d for a, b, d in zip(of_chain, of_own, of_old)],
+                lambda part, i: copy(yd, part, i).wait_send(),
+            )
+
+        def chained(yd, part, i):
+            w, q = part
+            return rcopy(s2.at[yd, w, q], s2.at[yd, w, q], c_send.at[i], c_recv.at[i], twin)
+
+        def passed(j):
+            by_pair(j, of_chain, lambda part, i: chained(yd, part, i).wait_send())
+            by_pair(
+                j, [a + b for a, b in zip(of_own, of_old)], lambda part, i: s2_copy(yd, part, i).wait_send()
+            )
 
         out(s1_copy, 2 * yd + 1 - core)
 
         @pl.when(yd != y)
         def _():
-            out(s2_copy, 2 * yd + core)
+            passed(2 * yd + core)
 
         return 0
 
@@ -503,20 +631,29 @@
     z_left(last, BLK // 2)
     for g in range(4):
         x_group(g).wait_send()
+    for k in range(5):
+        t_copy(k).wait_send()
     newest_copy().wait_send()
     newest_all().wait_send()
-    for i in range(2):
-        @pl.when(jnp.logical_not(is_self[i]))
-        def _():
-            meta_copy(i).wait_send()
-
-    for i in range(2):
-        @pl.when(jnp.logical_not(is_self[i]))
-        def _():
-            rcopy(meta, metas.at[i], m_send.at[i], m_recv.at[i], up).wait_recv()
+    for way in range(2):
+        gone = metas.at[pl.ds(0, NZ // 2 - way)]
+        rcopy(gone, gone, m_send.at[way], m_recv.at[way, 0], up).wait_send()
+
+    @pl.when(home)
+    def _():
+        q_sent(7).wait_send()
+        m_pair().wait_send()
+
+    @pl.when(jnp.logical_not(home))
+    def _():
+        q_sent(8).wait_send()
+
+    @pl.when(jnp.logical_not(home))
+    def _():
+        m_pair().wait_recv()
 
     lane = lax.broadcasted_iota(jnp.int32, (8, LANES), 1)
-    both = jnp.where(lane < BLK, metas[0], pltpu.roll(metas[1], BLK, 1))
+    both = jnp.where(lane < BLK, mpair[0], pltpu.roll(mpair[1], BLK, 1))
     q_inv = jnp.broadcast_to(1.0 / jnp.sqrt(both[0:1, :] + EPS), (LANES, LANES)).T
     q_ids = jnp.broadcast_to(both[1:2, :], (LANES, LANES)).T
     t_ids = tid_ref[...].astype(F32)
@@ -586,13 +723,17 @@
             pltpu.VMEM((4, 8, LANES, LANES), F32),
             pltpu.VMEM((4, 8, LANES, LANES), BF16),
             pltpu.VMEM((3, 8, LANES, LANES), BF16),
+            pltpu.VMEM((8, LANES, LANES), BF16),
             pltpu.VMEM((8, LANES, LANES), F32),
             pltpu.VMEM((8, LANES, LANES), BF16),
             pltpu.VMEM((2, 4, LANES, LANES), BF16),
             pltpu.VMEM((4, LANES, LANES), F32),
             pltpu.VMEM((8, LANES), F32),
-            pltpu.VMEM((16, 8, LANES), F32),
-            pltpu.VMEM((8, LANES), F32),
+            pltpu.VMEM((5, 8, LANES), F32),
+            pltpu.VMEM((2, 8, LANES), F32),
+            pltpu.VMEM((NZ, 8, LANES), F32),
+            pltpu.VMEM((16, 2, 8, LANES), F32),
+            pltpu.VMEM((2, 8, LANES), F32),
             pltpu.VMEM((2, 8, LANES), F32),
             pltpu.VMEM((8, LANES), F32),
             pltpu.VMEM((8, LANES), F32),
@@ -601,10 +742,11 @@
             dma((4,)), dma((4,)),
             dma((4, 5)), dma((4, 5)),
             dma((4, 5)), dma((5,)),
+            dma((1,)), dma((1,)), dma((1,)),
             dma, dma, dma, dma,
             dma((8,)), dma((2, 4)),
-            dma, dma,
-            dma((2,)), dma((2,)),
+            dma((5,)), dma((5,)),
+            dma((2,)), dma((2, NZ // 2 + 1)), dma, dma, dma, dma,
             dma, dma,
         ],
         compiler_params=pltpu.CompilerParams(

time: 86.2 us -> 86.3 us (level); the launches traced: 85 us -> 86.2 us
  Pallas kernels: 83.1 us -> 84.2 us
    pallas_call x1, Pallas kernels: 81.3 us -> 82.4 us  [shards(): pl.pallas_call(kernel, out_shape=(pltpu.VMEM((4, LANES, LANES), F32), plt...]
where the time goes in v4:
time: 86.3 us; the launch traced here: 86.2 us
  Pallas kernels  84.2 us (98%)
  local copies, waits for them, and re-layouts  1.31 us (2%)
    pallas_call x1, Pallas kernels, shards(): pl.pallas_call(kernel, out_shape=(pltpu.VMEM((4, LANES, LANES), F32), plt...  82.4 us
    pallas_call x1, Pallas kernels, shards(): pl.pallas_call(lay_out, out_shape=(jax.ShapeDtypeStruct((ROWS, LANES), F3...  1.79 us

profile of v4, /device:TPU:1, one launch (start us, length us, event | category | flops | bytes accessed | tf_op | source)
XLA Modules:
  0.0 86.2 jit_solution(1886722850673051590)
XLA Ops:
  0.6 82.4 %shard_map.86 = (f32[4,128,128]{2,1,0:T(8,128)S(1)}, f32[16,8,128]{2,1,0:T(8,128)S(1)}) custom-call(bf16[512,2048]{1,0:T(8,128)(2,1)} %tc_hbm.1, s32[16,512]{1,0:T(8,128)} %bitcast.6, s32[4,128]{1,0:T(4,128)} %bitcast.9, bf16[64,2048]{1,0:T(8,128)(2,1)} %qc_hbm.1, s32[16,64]{1,0:T(8,128)} %bitcast.7, s32[1,64]{1,0:T(1,128)} %bitcast.11, f32[16,128]{1,0:T(8,128)} %bitcast.8), custom_call_target="tpu_custom_call" | custom-call | flops 4294967296 | bytes 3145728 | tf_op jit(solution)/shard_map/pallas_call | solution.py:705
  83.1 0.0 copy-start
  83.1 0.7 copy-done
  83.8 0.0 copy-start.1
  83.8 0.6 copy-done.1
  84.4 1.8 %shard_map.87 = (f32[512,128]{1,0:T(8,128)}, f32[4,128]{1,0:T(4,128)}) custom-call(f32[4,128,128]{2,1,0:T(8,128)} %copy-done, f32[16,8,128]{2,1,0:T(8,128)} %copy-done.1), custom_call_target="tpu_custom_call" | custom-call | tf_op jit(solution)/shard_map/pallas_call | solution.py:762
Async XLA Ops:
  83.1 0.7 copy-start
  83.8 0.6 copy-start.1
